TPU v7x, 512 devices: a whole 4x4x16 slice. The times are simulated.
512 devices in a mesh: row: 64 (over y, z), col: 8 (over x, core).
Axes of the slice: x: 4, y: 4, z: 16, core: 2. Of those that a mesh axis runs over, the one named last changes fastest.
Arguments:
- inputs: bfloat16 [512, 8192], P(None, 'col'), may hold values from -6 to 6
- out_grad: bfloat16 [512, 8192], P(None, 'col'), may hold values from -6 to 6
- gate_weight: bfloat16 [8192, 16384], P('col', 'row'), may hold values from -0.0625 to 0.0625
- up_weight: bfloat16 [8192, 16384], P('col', 'row'), may hold values from -0.0625 to 0.0625
- down_weight: bfloat16 [16384, 8192], P('row', 'col'), may hold values from -0.046875 to 0.046875
Outputs:
- input_grad: bfloat16 [512, 8192], P('row', 'col')
- gate_wgrad: bfloat16 [8192, 16384], P('col', 'row')
- up_wgrad: bfloat16 [8192, 16384], P('col', 'row')
- down_wgrad: bfloat16 [16384, 8192], P('row', 'col')
All inputs are finite; a program needn't handle non-finite values.
Results may differ from a plain program's by a relative error of at most 0.005.
Values may be sent and summed in bfloat16 or wider, within the bound.
No kernel may reach another device: no remote copies, remote signals or barrier semaphores. Data moves between devices by JAX's collectives and lax.ppermute only.
A program may use at most 64 MiB of HBM per device.

v0:
```python
import math

import jax
import jax.numpy as jnp
from jax import lax
from jax.sharding import PartitionSpec as P

TOKENS = 512


def swiglu_back(gate, up, act_grad):
    sig = jax.nn.sigmoid(gate)
    hidden = (gate * sig * up).astype(jnp.bfloat16)
    up_grad = (act_grad * gate * sig).astype(jnp.bfloat16)
    gate_grad = (act_grad * up * sig * (1.0 + gate * (1.0 - sig))).astype(jnp.bfloat16)
    return (hidden, gate_grad, up_grad)


def weight_term(left, right, scale):
    return (
        lax.dot_general(left, right, (((0,), (0,)), ((), ())), preferred_element_type=jnp.float32)
        * scale
    ).astype(jnp.bfloat16)


def back_term(gate_grad, up_grad, gate_weight, up_weight):
    total = lax.dot_general(
        gate_grad, gate_weight, (((1,), (1,)), ((), ())), preferred_element_type=jnp.float32
    )
    return total + lax.dot_general(
        up_grad, up_weight, (((1,), (1,)), ((), ())), preferred_element_type=jnp.float32
    )


def per_device(inputs, out_grad, gate_weight, up_weight, down_weight):
    scale = 1.0 / math.sqrt(TOKENS)
    gate_part = jnp.dot(inputs, gate_weight, preferred_element_type=jnp.float32)
    up_part = jnp.dot(inputs, up_weight, preferred_element_type=jnp.float32)
    act_part = lax.dot_general(
        out_grad, down_weight, (((1,), (1,)), ((), ())), preferred_element_type=jnp.float32
    )
    gate, up, act_grad = lax.psum((gate_part, up_part, act_part), "col")
    hidden, gate_grad, up_grad = swiglu_back(gate, up, act_grad)
    down_wgrad = weight_term(hidden, out_grad, scale)
    gate_wgrad = weight_term(inputs, gate_grad, scale)
    up_wgrad = weight_term(inputs, up_grad, scale)
    terms = back_term(gate_grad, up_grad, gate_weight, up_weight)
    input_grad = lax.psum_scatter(terms, "row", scatter_dimension=0, tiled=True)
    return (input_grad.astype(jnp.bfloat16), gate_wgrad, up_wgrad, down_wgrad)


def solution(mesh):
    return jax.shard_map(
        per_device,
        mesh=mesh,
        in_specs=(
            P(None, "col"),
            P(None, "col"),
            P("col", "row"),
            P("col", "row"),
            P("row", "col"),
        ),
        out_specs=(P("row", "col"), P("col", "row"), P("col", "row"), P("row", "col")),
        check_vma=False,
    )
```

profile of v0, /device:TPU:2, one launch (start us, length us, event | category | flops | bytes accessed | tf_op | source)
XLA Modules:
  0.0 804.3 jit_solution(8277764977740716895)
XLA Ops:
  7.2 0.0 copy-start
  7.2 0.0 copy-start.2
  7.2 0.0 copy-start.3
  7.2 0.0 copy-start.4
  7.2 0.0 all-reduce.3.cloned.1.call-start
  7.3 1.1 copy-done
  8.4 2.3 fusion.8
  10.7 0.0 copy-done.2
  10.7 1.2 fusion.9
  11.9 0.0 copy-done.3
  11.9 0.0 copy-done.4
  11.9 1.3 fusion.7
  13.2 0.0 all-reduce.3.cloned.1.call-update
  13.2 0.0 reduce-scatter.2.cloned.1.call-start
  13.3 81.8 %all-reduce.3.cloned.1.call-done = (f32[512,256]{1,0:T(8,128)}, f32[512,256]{1,0:T(8,128)}, f32[512,256]{1,0:T(8,128)}) async-done(((f32[512,256]{1,0:T(8,128)}, f32[512,256]{1,0:T(8,128)}, f32[512,256]{1,0:T(8,128)}), (f32[512,256]{1,0:T(8,128)}, f32[512,256]{1,0:T(8,128)}, f32[512,256]{1,0:T(8,128)})) %all-reduce.3.cloned.1.call-update) | async-done | bytes 1572880 | tf_op jit(solution)/shard_map/psum | solution.py:42
  95.1 0.0 copy-start.1
  95.1 1.7 multiply_convert_fusion.1
  96.7 0.5 fusion.10
  97.2 0.0 copy-done.1
  97.2 1.8 convolution_add_fusion
  99.0 0.0 reduce-scatter.2.cloned.1.call-update
  99.1 0.5 fusion.3
  99.5 0.0 copy-start.5
  99.5 1.0 copy.10
  100.5 0.5 fusion.4
  101.0 1.0 copy.9
  102.0 0.0 copy-done.5
  102.0 2.3 fusion.2
  104.3 691.8 %reduce-scatter.2.cloned.1.call-done = f32[8,1024]{1,0:T(8,128)} async-done(((f32[512,1024]{1,0:T(8,128)}), f32[8,1024]{1,0:T(8,128)}) %reduce-scatter.2.cloned.1.call-update) | async-done | bytes 32784 | tf_op jit(solution)/shard_map/reduce_scatter | solution.py:48
  796.1 1.4 convert_element_type.29
Async XLA Ops:
  7.2 1.2 copy-start
  7.2 3.5 copy-start.2
  7.2 4.7 copy-start.3
  7.2 4.7 copy-start.4
  7.2 87.9 %all-reduce.3.cloned.1.call-start = ((), (), s32[]{:S(2)}) async-start(), calls=%async_computation.2 | async-start | bytes 3145728 | tf_op jit(solution)/shard_map/psum | solution.py:42
  13.2 782.9 %reduce-scatter.2.cloned.1.call-start = ((), (), s32[]{:S(2)}) async-start(), calls=%async_computation.1 | async-start | bytes 2129920 | tf_op jit(solution)/shard_map/reduce_scatter | solution.py:48
  95.1 2.1 copy-start.1
  99.5 2.5 copy-start.5
Sparse Core Ops, SparseCore 0:
  13.3 81.7 all-reduce.2
  99.5 696.5 reduce-scatter.1
where the time goes:
time: 805 us; the launch traced here: 804 us
  waiting for transfers between devices  774 us (96%)
  between operations  14.1 us (2%)
  matrix products  10.3 us (1%)
    reduce_scatter x1, waiting for transfers between devices, per_device(): input_grad = lax.psum_scatter(terms, 'row', scatter_dimension=0, tiled=True)  692 us
    psum x1, waiting for transfers between devices, per_device(): gate, up, act_grad = lax.psum((gate_part, up_part, act_part), 'col')  81.8 us
  transfers between devices with their start and end apart: 2, of which 2 were waited for; matrix products, arithmetic and copies ran while one was open for 1% of the time, Pallas kernels for 0%

commit v1 on v0

--- a/solution.py
+++ b/solution.py
@@ -3,9 +3,11 @@
 import jax
 import jax.numpy as jnp
 from jax import lax
-from jax.sharding import PartitionSpec as P
+from jax.sharding import Mesh, PartitionSpec as P
 
 TOKENS = 512
+COL = ("x", "core")
+ROW = ("y", "z")
 
 
 def swiglu_back(gate, up, act_grad):
@@ -32,6 +34,12 @@
     )
 
 
+def sum_scatter(terms, axis, parts):
+    rows = terms.shape[0] // parts
+    pieces = lax.all_to_all(terms.reshape((parts, rows) + terms.shape[1:]), axis, 0, 0)
+    return jnp.sum(pieces.astype(jnp.float32), axis=0)
+
+
 def per_device(inputs, out_grad, gate_weight, up_weight, down_weight):
     scale = 1.0 / math.sqrt(TOKENS)
     gate_part = jnp.dot(inputs, gate_weight, preferred_element_type=jnp.float32)
@@ -39,27 +47,31 @@
     act_part = lax.dot_general(
         out_grad, down_weight, (((1,), (1,)), ((), ())), preferred_element_type=jnp.float32
     )
-    gate, up, act_grad = lax.psum((gate_part, up_part, act_part), "col")
-    hidden, gate_grad, up_grad = swiglu_back(gate, up, act_grad)
+    units = gate_part.shape[1]
+    parts = jnp.concatenate([gate_part, up_part, act_part], axis=1).astype(jnp.bfloat16)
+    sums = sum_scatter(parts, COL, 8)
+    own = swiglu_back(sums[:, :units], sums[:, units : 2 * units], sums[:, 2 * units :])
+    whole = lax.all_gather(jnp.concatenate(own, axis=1), COL, axis=0, tiled=True)
+    hidden, gate_grad, up_grad = (
+        whole[:, :units],
+        whole[:, units : 2 * units],
+        whole[:, 2 * units :],
+    )
+    terms = back_term(gate_grad, up_grad, gate_weight, up_weight).astype(jnp.bfloat16)
+    near = sum_scatter(terms, "y", 4).astype(jnp.bfloat16)
+    input_grad = sum_scatter(near, "z", 16)
     down_wgrad = weight_term(hidden, out_grad, scale)
     gate_wgrad = weight_term(inputs, gate_grad, scale)
     up_wgrad = weight_term(inputs, up_grad, scale)
-    terms = back_term(gate_grad, up_grad, gate_weight, up_weight)
-    input_grad = lax.psum_scatter(terms, "row", scatter_dimension=0, tiled=True)
     return (input_grad.astype(jnp.bfloat16), gate_wgrad, up_wgrad, down_wgrad)
 
 
 def solution(mesh):
+    grid = Mesh(mesh.devices.reshape(4, 16, 4, 2), ("y", "z", "x", "core"))
     return jax.shard_map(
         per_device,
-        mesh=mesh,
-        in_specs=(
-            P(None, "col"),
-            P(None, "col"),
-            P("col", "row"),
-            P("col", "row"),
-            P("row", "col"),
-        ),
-        out_specs=(P("row", "col"), P("col", "row"), P("col", "row"), P("row", "col")),
+        mesh=grid,
+        in_specs=(P(None, COL), P(None, COL), P(COL, ROW), P(COL, ROW), P(ROW, COL)),
+        out_specs=(P(ROW, COL), P(COL, ROW), P(COL, ROW), P(ROW, COL)),
         check_vma=False,
     )

time: 805 us -> 91.1 us (0.11)
  the two profiles are of different devices: /device:TPU:2 before, /device:TPU:64 now
where the time goes in v1:
time: 91.1 us; the launch traced here: 90.8 us
  blocking collectives  50.7 us (56%)
  starting transfers between devices  14.8 us (16%)
  waiting for transfers between devices  12.8 us (14%)
  matrix products  6.79 us (7%)
  local copies, waits for them, and re-layouts  3.22 us (4%)
  other arithmetic  1.78 us (2%)
    all_to_all x2, blocking collectives, sum_scatter(): lax.all_to_all(terms.reshape((parts, rows) + terms.shape[1:]), axis, 0, 0)  37.2 us
    all_to_all x1, starting transfers between devices, sum_scatter(): lax.all_to_all(terms.reshape((parts, rows) + terms.shape[1:]), axis, 0, 0)  14.8 us
    all_gather x1, blocking collectives, per_device(): lax.all_gather(jnp.concatenate(own, axis=1), COL, axis=0, tiled=True)  13.5 us
    all_to_all x1, waiting for transfers between devices, sum_scatter(): lax.all_to_all(terms.reshape((parts, rows) + terms.shape[1:]), axis, 0, 0)  12.8 us
    dot_general x3, matrix products, weight_term(): lax.dot_general(left, right, (((0,), (0,)), ((), ())), preferred_element_...  3.4 us
    unnamed x12, local copies, waits for them, and re-layouts  3.22 us
  transfers between devices with their start and end apart: 1, of which 1 were waited for; matrix products, arithmetic and copies ran while one was open for 6% of the time, Pallas kernels for 0%

profile of v1, /device:TPU:64, one launch (start us, length us, event | category | flops | bytes accessed | tf_op | source)
XLA Modules:
  0.0 90.8 jit_solution(5022061470203406685)
XLA Ops:
  0.6 0.0 copy-start
  0.6 0.0 copy-start.1
  0.7 0.0 copy-start.3
  0.7 1.2 %copy-done = bf16[512,1024]{1,0:T(8,128)(2,1)S(1)} copy-done((bf16[512,1024]{1,0:T(8,128)(2,1)S(1)}, bf16[512,1024]{1,0:T(8,128)(2,1)}, u32[]{:S(2)}) %copy-start) | copy-done | bytes 1048600
  1.9 0.0 copy-start.4
  1.9 1.5 %convolution_convert_fusion.2 = bf16[512,256]{1,0:T(8,128)(2,1)S(1)} fusion(bf16[512,1024]{1,0:T(8,128)(2,1)S(1)} %copy-done, bf16[1024,256]{1,0:T(8,128)(2,1)} %param.7), kind=kOutput, calls=%fused_computation.12 | convolution fusion | flops 268566528 | bytes 1835008 | tf_op jit(solution)/shard_map/dot_general | solution.py:45
  3.4 0.0 copy-done.1
  3.4 0.4 convolution_convert_fusion.1
  3.9 0.0 copy-done.3
  3.9 0.0 copy-done.4
  3.9 0.5 convolution_convert_fusion
  4.4 0.1 pad_maximum_fusion
  4.4 17.4 %all_to_all.15 = bf16[8,64,768]{2,1,0:T(8,128)(2,1)S(1)} all-to-all(bf16[8,64,768]{2,1,0:T(8,128)(2,1)S(1)} %pad_maximum_fusion), channel_id=1, replica_groups=mesh['y'=4,'z'=16,'x'=4,'core'=2] {'x','core'}, dimensions={0} | all-to-all | bytes 1572864 | tf_op jit(solution)/shard_map/all_to_all | solution.py:39
  21.8 0.0 copy-start.2
  21.8 0.1 convert_reduce_fusion
  21.9 13.5 %all_gather.3 = bf16[512,768]{1,0:T(8,128)(2,1)S(1)} all-gather(bf16[64,768]{1,0:T(8,128)(2,1)S(1)} %pad_maximum_fusion.1), channel_id=1, replica_groups=mesh['y'=4,'z'=16,'x'=4,'core'=2] {'x','core'}, dimensions={0}, use_global_device_ids=true | all-gather | bytes 884736 | tf_op jit(solution)/shard_map/all_gather | solution.py:54
  35.4 0.0 copy-done.2
  35.4 0.5 fusion.9
  35.9 0.5 add_convert_fusion
  36.4 19.9 %all_to_all.16 = bf16[4,128,1024]{2,1,0:T(8,128)(2,1)S(1)} all-to-all(bf16[4,128,1024]{2,1,0:T(8,128)(2,1)S(1)} %bitcast.20), channel_id=1, replica_groups=mesh['y'=4,'z'=16,'x'=4,'core'=2] {'y'}, dimensions={0} | all-to-all | bytes 2097152 | tf_op jit(solution)/shard_map/all_to_all | solution.py:39
  56.2 0.9 %reduce_sum.34 = bf16[128,1024]{1,0:T(8,128)(2,1)} reduce(bf16[4,128,1024]{2,1,0:T(8,128)(2,1)S(1)} %all_to_all.16, bf16[]{:T(256)} %constant.8.clone.1), dimensions={0}, to_apply=%region_1.0 | reduce | flops 393216 | bytes 1310722 | tf_op jit(solution)/shard_map/reduce_sum | solution.py:40
  57.2 14.8 %all-to-all-start.2 = ((bf16[16,8,1024]{2,1,0:T(8,128)(2,1)}), bf16[16,8,1024]{2,1,0:T(8,128)(2,1)S(1)}, u32[]{:S(2)}, u32[]{:S(2)}) async-start(bf16[16,8,1024]{2,1,0:T(8,128)(2,1)} %bitcast.4), calls=%async_computation.2 | async-start | bytes 524288 | tf_op jit(solution)/shard_map/all_to_all | solution.py:39
  71.9 0.5 fusion.4
  72.4 1.0 %copy.11 = bf16[1024,256]{1,0:T(8,128)(2,1)} copy(bf16[1024,256]{0,1:T(8,128)(2,1)S(1)} %fusion.4) | data formatting | bytes 1048576
  73.4 0.5 fusion.3
  73.8 1.0 %copy.12 = bf16[1024,256]{1,0:T(8,128)(2,1)} copy(bf16[1024,256]{0,1:T(8,128)(2,1)S(1)} %fusion.3) | data formatting | bytes 1048576
  74.8 2.5 %fusion.2 = bf16[256,1024]{1,0:T(8,128)(2,1)} fusion(bf16[512,1024]{1,0:T(8,128)(2,1)} %param.6, bf16[512,768]{1,0:T(8,128)(2,1)S(1)} %all_gather.3), kind=kOutput, calls=%fused_computation.7 | convolution fusion | flops 268959744 | bytes 1835008 | tf_op jit(solution)/shard_map/dot_general | solution.py:23
  77.3 12.8 %all-to-all-done.2 = bf16[16,8,1024]{2,1,0:T(8,128)(2,1)S(1)} async-done(((bf16[16,8,1024]{2,1,0:T(8,128)(2,1)}), bf16[16,8,1024]{2,1,0:T(8,128)(2,1)S(1)}, u32[]{:S(2)}, u32[]{:S(2)}) %all-to-all-start.2) | async-done | bytes 262176 | tf_op jit(solution)/shard_map/all_to_all | solution.py:39
  90.1 0.6 reduce_sum.35
  (2 shorter events, 0.1 us)
Async XLA Ops:
  0.6 1.2 %copy-start = (bf16[512,1024]{1,0:T(8,128)(2,1)S(1)}, bf16[512,1024]{1,0:T(8,128)(2,1)}, u32[]{:S(2)}) copy-start(bf16[512,1024]{1,0:T(8,128)(2,1)} %param.5) | copy-start | bytes 3145732
  0.6 2.8 %copy-start.1 = (bf16[1024,256]{1,0:T(8,128)(2,1)S(1)}, bf16[1024,256]{1,0:T(8,128)(2,1)}, u32[]{:S(2)}) copy-start(bf16[1024,256]{1,0:T(8,128)(2,1)} %param.8) | copy-start | bytes 1572868
  0.7 3.2 %copy-start.3 = (bf16[512,1024]{1,0:T(8,128)(2,1)S(1)}, bf16[512,1024]{1,0:T(8,128)(2,1)}, u32[]{:S(2)}) copy-start(bf16[512,1024]{1,0:T(8,128)(2,1)} %param.6) | copy-start | bytes 3145732
  1.9 2.0 %copy-start.4 = (bf16[256,1024]{1,0:T(8,128)(2,1)S(1)}, bf16[256,1024]{1,0:T(8,128)(2,1)}, u32[]{:S(2)}) copy-start(bf16[256,1024]{1,0:T(8,128)(2,1)} %param.9) | copy-start | bytes 1572868
  21.8 13.7 %copy-start.2 = (bf16[1024,256]{1,0:T(8,128)(2,1)S(1)}, bf16[1024,256]{1,0:T(8,128)(2,1)}, u32[]{:S(2)}) copy-start(bf16[1024,256]{1,0:T(8,128)(2,1)} %param.7) | copy-start | bytes 1572868
  57.2 33.0 %all-to-all-start.2 = ((bf16[16,8,1024]{2,1,0:T(8,128)(2,1)}), bf16[16,8,1024]{2,1,0:T(8,128)(2,1)S(1)}, u32[]{:S(2)}, u32[]{:S(2)}) async-start(bf16[16,8,1024]{2,1,0:T(8,128)(2,1)} %bitcast.4), calls=%async_computation.2 | async-start | bytes 524288 | tf_op jit(solution)/shard_map/all_to_all | solution.py:39

commit v2 on v1

--- a/solution.py
+++ b/solution.py
@@ -7,7 +7,7 @@
 
 TOKENS = 512
 COL = ("x", "core")
-ROW = ("y", "z")
+ROW = ("y", "zhigh", "zlow")
 
 
 def swiglu_back(gate, up, act_grad):
@@ -40,6 +40,11 @@
     return jnp.sum(pieces.astype(jnp.float32), axis=0)
 
 
+def by_pair(rows):
+    parts = rows.reshape((4, 8, 2, 8) + rows.shape[1:])
+    return jnp.swapaxes(parts, 1, 2).reshape(rows.shape)
+
+
 def per_device(inputs, out_grad, gate_weight, up_weight, down_weight):
     scale = 1.0 / math.sqrt(TOKENS)
     gate_part = jnp.dot(inputs, gate_weight, preferred_element_type=jnp.float32)
@@ -57,9 +62,9 @@
         whole[:, units : 2 * units],
         whole[:, 2 * units :],
     )
-    terms = back_term(gate_grad, up_grad, gate_weight, up_weight).astype(jnp.bfloat16)
-    near = sum_scatter(terms, "y", 4).astype(jnp.bfloat16)
-    input_grad = sum_scatter(near, "z", 16)
+    terms = back_term(by_pair(gate_grad), by_pair(up_grad), gate_weight, up_weight)
+    near = sum_scatter(terms.astype(jnp.bfloat16), ("y", "zlow"), 8).astype(jnp.bfloat16)
+    input_grad = sum_scatter(near, "zhigh", 8)
     down_wgrad = weight_term(hidden, out_grad, scale)
     gate_wgrad = weight_term(inputs, gate_grad, scale)
     up_wgrad = weight_term(inputs, up_grad, scale)
@@ -67,7 +72,7 @@
 
 
 def solution(mesh):
-    grid = Mesh(mesh.devices.reshape(4, 16, 4, 2), ("y", "z", "x", "core"))
+    grid = Mesh(mesh.devices.reshape(4, 8, 2, 4, 2), ("y", "zhigh", "zlow", "x", "core"))
     return jax.shard_map(
         per_device,
         mesh=grid,

time: 91.1 us -> 89.9 us (0.987)
  the two profiles are of different devices: /device:TPU:64 before, /device:TPU:32 now
where the time goes in v2:
time: 89.9 us; the launch traced here: 89.6 us
  blocking collectives  31 us (34%)
  waiting for transfers between devices  26.5 us (29%)
  starting transfers between devices  19.8 us (22%)
  matrix products  6.53 us (7%)
  local copies, waits for them, and re-layouts  3.3 us (4%)
  other arithmetic  1.67 us (2%)
    all_to_all x2, waiting for transfers between devices, sum_scatter(): lax.all_to_all(terms.reshape((parts, rows) + terms.shape[1:]), axis, 0, 0)  26.5 us
    all_to_all x2, starting transfers between devices, sum_scatter(): lax.all_to_all(terms.reshape((parts, rows) + terms.shape[1:]), axis, 0, 0)  19.8 us
    all_to_all x1, blocking collectives, sum_scatter(): lax.all_to_all(terms.reshape((parts, rows) + terms.shape[1:]), axis, 0, 0)  17.3 us
    all_gather x1, blocking collectives, per_device(): lax.all_gather(jnp.concatenate(own, axis=1), COL, axis=0, tiled=True)  13.6 us
    unnamed x14, local copies, waits for them, and re-layouts  3.23 us
    dot_general x3, matrix products, weight_term(): lax.dot_general(left, right, (((0,), (0,)), ((), ())), preferred_element_...  2.18 us
  transfers between devices with their start and end apart: 2, of which 2 were waited for; matrix products, arithmetic and copies ran while one was open for 5% of the time, Pallas kernels for 0%

profile of v2, /device:TPU:32, one launch (start us, length us, event | category | flops | bytes accessed | tf_op | source)
XLA Modules:
  0.0 89.6 jit_solution(1447235280691754359)
XLA Ops:
  0.6 0.0 copy-start
  0.6 0.0 copy-start.1
  0.7 0.0 copy-start.3
  0.7 1.2 %copy-done = bf16[512,1024]{1,0:T(8,128)(2,1)S(1)} copy-done((bf16[512,1024]{1,0:T(8,128)(2,1)S(1)}, bf16[512,1024]{1,0:T(8,128)(2,1)}, u32[]{:S(2)}) %copy-start) | copy-done | bytes 1048600
  1.9 0.0 copy-start.5
  1.9 1.5 %convolution_convert_fusion.2 = bf16[512,256]{1,0:T(8,128)(2,1)S(1)} fusion(bf16[512,1024]{1,0:T(8,128)(2,1)S(1)} %copy-done, bf16[1024,256]{1,0:T(8,128)(2,1)} %param.7), kind=kOutput, calls=%fused_computation.12 | convolution fusion | flops 268566528 | bytes 1835008 | tf_op jit(solution)/shard_map/dot_general | solution.py:50
  3.4 0.0 copy-done.1
  3.4 0.4 convolution_convert_fusion.1
  3.9 0.0 copy-done.3
  3.9 0.0 copy-done.5
  3.9 0.5 convolution_convert_fusion
  4.4 0.1 pad_maximum_fusion
  4.4 17.3 %all_to_all.15 = bf16[8,64,768]{2,1,0:T(8,128)(2,1)S(1)} all-to-all(bf16[8,64,768]{2,1,0:T(8,128)(2,1)S(1)} %pad_maximum_fusion), channel_id=1, replica_groups=mesh['y'=4,'zhigh'=8,'zlow'=2,'x'=4,'core'=2] {'x','core'}, dimensions={0} | all-to-all | bytes 1572864 | tf_op jit(solution)/shard_map/all_to_all | solution.py:39
  21.8 0.1 convert_reduce_fusion
  21.9 0.0 copy-start.2
  22.0 13.6 %all_gather.3 = bf16[512,768]{1,0:T(8,128)(2,1)S(1)} all-gather(bf16[64,768]{1,0:T(8,128)(2,1)S(1)} %pad_maximum_fusion.1), channel_id=1, replica_groups=mesh['y'=4,'zhigh'=8,'zlow'=2,'x'=4,'core'=2] {'x','core'}, dimensions={0}, use_global_device_ids=true | all-gather | bytes 884736 | tf_op jit(solution)/shard_map/all_gather | solution.py:59
  35.6 0.0 copy-done.2
  35.6 0.5 fusion.9
  36.1 1.4 %add_convert_fusion = bf16[512,1024]{1,0:T(8,128)(2,1)} fusion(f32[512,1024]{1,0:T(8,128)S(1)} %fusion.9, bf16[512,256]{1,0:T(8,128)(2,1)S(1)} %bitcast.33, bf16[1024,256]{1,0:T(8,128)(2,1)S(1)} %copy-done.1), kind=kOutput, calls=%fused_computation | convolution fusion | flops 269484032 | bytes 3932160 | tf_op jit(solution)/shard_map/dot_general | solution.py:32
  37.6 7.3 %all-to-all-start.1 = ((bf16[8,64,1024]{2,1,0:T(8,128)(2,1)}), bf16[8,64,1024]{2,1,0:T(8,128)(2,1)S(1)}, u32[]{:S(2)}, u32[]{:S(2)}) async-start(bf16[8,64,1024]{2,1,0:T(8,128)(2,1)} %bitcast.9), calls=%async_computation.1 | async-start | bytes 2097152 | tf_op jit(solution)/shard_map/all_to_all | solution.py:39
  44.8 0.5 fusion.4
  45.3 1.0 %copy.19 = bf16[1024,256]{1,0:T(8,128)(2,1)} copy(bf16[1024,256]{0,1:T(8,128)(2,1)S(1)} %fusion.4) | data formatting | bytes 1048576
  46.3 13.9 %all-to-all-done.1 = bf16[8,64,1024]{2,1,0:T(8,128)(2,1)S(1)} async-done(((bf16[8,64,1024]{2,1,0:T(8,128)(2,1)}), bf16[8,64,1024]{2,1,0:T(8,128)(2,1)S(1)}, u32[]{:S(2)}, u32[]{:S(2)}) %all-to-all-start.1) | async-done | bytes 1048608 | tf_op jit(solution)/shard_map/all_to_all | solution.py:39
  60.2 0.8 reduce_sum.34
  61.0 12.6 %all-to-all-start.2 = ((bf16[8,8,1024]{2,1,0:T(8,128)(2,1)}), bf16[8,8,1024]{2,1,0:T(8,128)(2,1)S(1)}, u32[]{:S(2)}, u32[]{:S(2)}) async-start(bf16[8,8,1024]{2,1,0:T(8,128)(2,1)} %bitcast.10), calls=%async_computation.2 | async-start | bytes 262144 | tf_op jit(solution)/shard_map/all_to_all | solution.py:39
  73.6 0.0 copy-start.4
  73.6 0.5 fusion.3
  74.0 1.0 %copy.20 = bf16[1024,256]{1,0:T(8,128)(2,1)} copy(bf16[1024,256]{0,1:T(8,128)(2,1)S(1)} %fusion.3) | data formatting | bytes 1048576
  75.0 0.0 copy-done.4
  75.0 1.3 %fusion.2 = bf16[256,1024]{1,0:T(8,128)(2,1)} fusion(bf16[512,1024]{1,0:T(8,128)(2,1)S(1)} %copy-done.4, bf16[512,768]{1,0:T(8,128)(2,1)S(1)} %all_gather.3), kind=kOutput, calls=%fused_computation.7 | convolution fusion | flops 268959744 | bytes 1835008 | tf_op jit(solution)/shard_map/dot_general | solution.py:23
  76.3 12.6 %all-to-all-done.2 = bf16[8,8,1024]{2,1,0:T(8,128)(2,1)S(1)} async-done(((bf16[8,8,1024]{2,1,0:T(8,128)(2,1)}), bf16[8,8,1024]{2,1,0:T(8,128)(2,1)S(1)}, u32[]{:S(2)}, u32[]{:S(2)}) %all-to-all-start.2) | async-done | bytes 131104 | tf_op jit(solution)/shard_map/all_to_all | solution.py:39
  89.0 0.6 reduce_sum.35
  (5 shorter events, 0.1 us)
Async XLA Ops:
  0.6 1.2 %copy-start = (bf16[512,1024]{1,0:T(8,128)(2,1)S(1)}, bf16[512,1024]{1,0:T(8,128)(2,1)}, u32[]{:S(2)}) copy-start(bf16[512,1024]{1,0:T(8,128)(2,1)} %param.5) | copy-start | bytes 3145732
  0.6 2.8 %copy-start.1 = (bf16[1024,256]{1,0:T(8,128)(2,1)S(1)}, bf16[1024,256]{1,0:T(8,128)(2,1)}, u32[]{:S(2)}) copy-start(bf16[1024,256]{1,0:T(8,128)(2,1)} %param.8) | copy-start | bytes 1572868
  0.7 3.2 %copy-start.3 = (bf16[512,1024]{1,0:T(8,128)(2,1)S(1)}, bf16[512,1024]{1,0:T(8,128)(2,1)}, u32[]{:S(2)}) copy-start(bf16[512,1024]{1,0:T(8,128)(2,1)} %param.6) | copy-start | bytes 3145732
  1.9 2.0 %copy-start.5 = (bf16[256,1024]{1,0:T(8,128)(2,1)S(1)}, bf16[256,1024]{1,0:T(8,128)(2,1)}, u32[]{:S(2)}) copy-start(bf16[256,1024]{1,0:T(8,128)(2,1)} %param.9) | copy-start | bytes 1572868
  21.9 13.8 %copy-start.2 = (bf16[1024,256]{1,0:T(8,128)(2,1)S(1)}, bf16[1024,256]{1,0:T(8,128)(2,1)}, u32[]{:S(2)}) copy-start(bf16[1024,256]{1,0:T(8,128)(2,1)} %param.7) | copy-start | bytes 1572868
  37.6 22.6 %all-to-all-start.1 = ((bf16[8,64,1024]{2,1,0:T(8,128)(2,1)}), bf16[8,64,1024]{2,1,0:T(8,128)(2,1)S(1)}, u32[]{:S(2)}, u32[]{:S(2)}) async-start(bf16[8,64,1024]{2,1,0:T(8,128)(2,1)} %bitcast.9), calls=%async_computation.1 | async-start | bytes 2097152 | tf_op jit(solution)/shard_map/all_to_all | solution.py:39
  61.0 27.9 %all-to-all-start.2 = ((bf16[8,8,1024]{2,1,0:T(8,128)(2,1)}), bf16[8,8,1024]{2,1,0:T(8,128)(2,1)S(1)}, u32[]{:S(2)}, u32[]{:S(2)}) async-start(bf16[8,8,1024]{2,1,0:T(8,128)(2,1)} %bitcast.10), calls=%async_computation.2 | async-start | bytes 262144 | tf_op jit(solution)/shard_map/all_to_all | solution.py:39
  73.6 1.5 %copy-start.4 = (bf16[512,1024]{1,0:T(8,128)(2,1)S(1)}, bf16[512,1024]{1,0:T(8,128)(2,1)}, u32[]{:S(2)}) copy-start(bf16[512,1024]{1,0:T(8,128)(2,1)} %param.6) | copy-start | bytes 3145732

commit v3 on v2

v3 whole, which is shorter than its diff:
```python
import math

import jax
import jax.numpy as jnp
from jax import lax
from jax.experimental import pallas as pl
from jax.experimental.pallas import tpu as pltpu
from jax.sharding import Mesh, PartitionSpec as P

TOKENS = 512
COL = ("x", "core")
ROW = ("y", "zhigh", "zlow")
CHUNKS = 4
NT = (((1,), (1,)), ((), ()))


def swiglu_back(gate, up, act_grad):
    sig = jax.nn.sigmoid(gate)
    hidden = (gate * sig * up).astype(jnp.bfloat16)
    up_grad = (act_grad * gate * sig).astype(jnp.bfloat16)
    gate_grad = (act_grad * up * sig * (1.0 + gate * (1.0 - sig))).astype(jnp.bfloat16)
    return (hidden, gate_grad, up_grad)


def weight_term(left, right, scale):
    return (
        lax.dot_general(left, right, (((0,), (0,)), ((), ())), preferred_element_type=jnp.float32)
        * scale
    ).astype(jnp.bfloat16)


def forward_kernel(x_hbm, o_hbm, g_hbm, u_hbm, d_hbm, out, x, o, g, u, d, sems):
    rows = x.shape[0] // CHUNKS
    units = g.shape[1]

    def copy(src, dst, sem):
        return pltpu.make_async_copy(src, dst, sems.at[sem])

    def part(i):
        return pl.ds(i * rows, rows)

    weights = [copy(g_hbm, g, 0), copy(u_hbm, u, 1), copy(d_hbm, d, 2)]
    lefts = [copy(x_hbm.at[part(i)], x.at[part(i)], 3 + i) for i in range(CHUNKS)]
    outs = [copy(o_hbm.at[part(i)], o.at[part(i)], 3 + CHUNKS + i) for i in range(CHUNKS)]
    for c in [weights[0], lefts[0], weights[1], *lefts[1:], weights[2], *outs]:
        c.start()
    for i in range(CHUNKS):
        lefts[i].wait()
        if i == 0:
            weights[0].wait()
        out[part(i), :units] = jnp.dot(
            x[part(i)], g[...], preferred_element_type=jnp.float32
        ).astype(jnp.bfloat16)
        if i == 0:
            weights[1].wait()
        out[part(i), units : 2 * units] = jnp.dot(
            x[part(i)], u[...], preferred_element_type=jnp.float32
        ).astype(jnp.bfloat16)
    weights[2].wait()
    for i in range(CHUNKS):
        outs[i].wait()
        out[part(i), 2 * units :] = lax.dot_general(
            o[part(i)], d[...], NT, preferred_element_type=jnp.float32
        ).astype(jnp.bfloat16)


def forward(inputs, out_grad, gate_weight, up_weight, down_weight):
    tokens, units = inputs.shape[0], gate_weight.shape[1]
    arrays = (inputs, out_grad, gate_weight, up_weight, down_weight)
    return pl.pallas_call(
        forward_kernel,
        out_shape=jax.ShapeDtypeStruct((tokens, 3 * units), jnp.bfloat16),
        in_specs=[pl.BlockSpec(memory_space=pl.ANY)] * 5,
        out_specs=pl.BlockSpec(memory_space=pltpu.VMEM),
        scratch_shapes=[pltpu.VMEM(a.shape, a.dtype) for a in arrays]
        + [pltpu.SemaphoreType.DMA((3 + 2 * CHUNKS,))],
        compiler_params=pltpu.CompilerParams(vmem_limit_bytes=56 << 20),
        cost_estimate=pl.CostEstimate(
            flops=6 * tokens * units * inputs.shape[1], bytes_accessed=4500000, transcendentals=0
        ),
        name="forward",
    )(*arrays)


def back_kernel(whole, g, u, out):
    units = g.shape[1]
    step = 256
    for j in range(g.shape[0] // step):
        cols = slice(j * step, (j + 1) * step)
        terms = lax.dot_general(
            whole[:, units : 2 * units], g[cols], NT, preferred_element_type=jnp.float32
        )
        terms += lax.dot_general(
            whole[:, 2 * units :], u[cols], NT, preferred_element_type=jnp.float32
        )
        terms = jnp.swapaxes(terms.reshape(4, 8, 2, 8, step), 1, 2)
        out[:, cols] = terms.reshape(-1, step).astype(jnp.bfloat16)


def back(whole, gate_weight, up_weight):
    tokens, width = whole.shape[0], gate_weight.shape[0]
    return pl.pallas_call(
        back_kernel,
        out_shape=jax.ShapeDtypeStruct((tokens, width), jnp.bfloat16),
        in_specs=[pl.BlockSpec(memory_space=pltpu.VMEM)] * 3,
        out_specs=pl.BlockSpec(memory_space=pltpu.VMEM),
        compiler_params=pltpu.CompilerParams(vmem_limit_bytes=24 << 20),
        cost_estimate=pl.CostEstimate(
            flops=4 * tokens * gate_weight.size, bytes_accessed=2500000, transcendentals=0
        ),
        name="back",
    )(whole, gate_weight, up_weight)


def sum_scatter(terms, axis, parts):
    rows = terms.shape[0] // parts
    pieces = lax.all_to_all(terms.reshape((parts, rows) + terms.shape[1:]), axis, 0, 0)
    return jnp.sum(pieces.astype(jnp.float32), axis=0)


def per_device(inputs, out_grad, gate_weight, up_weight, down_weight):
    scale = 1.0 / math.sqrt(TOKENS)
    units = gate_weight.shape[1]
    parts = forward(inputs, out_grad, gate_weight, up_weight, down_weight)
    sums = sum_scatter(parts, COL, 8)
    own = swiglu_back(sums[:, :units], sums[:, units : 2 * units], sums[:, 2 * units :])
    whole = lax.all_gather(jnp.concatenate(own, axis=1), COL, axis=0, tiled=True)
    terms = back(whole, gate_weight, up_weight)
    near = sum_scatter(terms, ("y", "zlow"), 8).astype(jnp.bfloat16)
    whole, near = lax.optimization_barrier((whole, near))
    input_grad = sum_scatter(near, "zhigh", 8)
    down_wgrad = weight_term(whole[:, :units], out_grad, scale)
    gate_wgrad = weight_term(inputs, whole[:, units : 2 * units], scale)
    up_wgrad = weight_term(inputs, whole[:, 2 * units :], scale)
    return (input_grad.astype(jnp.bfloat16), gate_wgrad, up_wgrad, down_wgrad)


def solution(mesh):
    grid = Mesh(mesh.devices.reshape(4, 8, 2, 4, 2), ("y", "zhigh", "zlow", "x", "core"))
    return jax.shard_map(
        per_device,
        mesh=grid,
        in_specs=(P(None, COL), P(None, COL), P(COL, ROW), P(COL, ROW), P(ROW, COL)),
        out_specs=(P(ROW, COL), P(COL, ROW), P(COL, ROW), P(ROW, COL)),
        check_vma=False,
    )
```

time: 89.9 us -> 89.7 us (level)
  the two profiles are of different devices: /device:TPU:32 before, /device:TPU:8 now
where the time goes in v3:
time: 89.7 us; the launch traced here: 89.4 us
  blocking collectives  53.1 us (59%)
  starting transfers between devices  12.8 us (14%)
  waiting for transfers between devices  11 us (12%)
  Pallas kernels  6.04 us (7%)
  matrix products  2.18 us (2%)
  local copies, waits for them, and re-layouts  2.01 us (2%)
  other arithmetic  1.61 us (2%)
    all_to_all x2, blocking collectives, sum_scatter(): lax.all_to_all(terms.reshape((parts, rows) + terms.shape[1:]), axis, 0, 0)  39.5 us
    all_gather x1, blocking collectives, per_device(): lax.all_gather(jnp.concatenate(own, axis=1), COL, axis=0, tiled=True)  13.6 us
    all_to_all x1, starting transfers between devices, sum_scatter(): lax.all_to_all(terms.reshape((parts, rows) + terms.shape[1:]), axis, 0, 0)  12.8 us
    all_to_all x1, waiting for transfers between devices, sum_scatter(): lax.all_to_all(terms.reshape((parts, rows) + terms.shape[1:]), axis, 0, 0)  11 us
    pallas_call x1, Pallas kernels, forward(): pl.pallas_call(forward_kernel, out_shape=jax.ShapeDtypeStruct((tokens, 3...  5.3 us
    dot_general x3, matrix products, weight_term(): lax.dot_general(left, right, (((0,), (0,)), ((), ())), preferred_element_...  2.18 us
    unnamed x10, local copies, waits for them, and re-layouts  2.01 us
  transfers between devices with their start and end apart: 1, of which 1 were waited for; matrix products, arithmetic and copies ran while one was open for 5% of the time, Pallas kernels for 0%

profile of v3, /device:TPU:8, one launch (start us, length us, event | category | flops | bytes accessed | tf_op | source)
XLA Modules:
  0.0 89.4 jit_solution(1720568890208235869)
XLA Ops:
  0.6 5.3 %forward.1 = bf16[512,768]{1,0:T(8,128)(2,1)} custom-call(bf16[512,1024]{1,0:T(8,128)(2,1)} %x_hbm.1, bf16[512,1024]{1,0:T(8,128)(2,1)} %o_hbm.1, bf16[1024,256]{1,0:T(8,128)(2,1)} %g.1, bf16[1024,256]{1,0:T(8,128)(2,1)} %u.1, bf16[256,1024]{1,0:T(8,128)(2,1)} %d_hbm.1), custom_call_target="tpu_custom_call" | custom-call | flops 805306368 | bytes 4500000 | tf_op jit(solution)/shard_map/forward/pallas_call | solution.py:70
  5.9 17.6 %all_to_all.15 = bf16[8,64,768]{2,1,0:T(8,128)(2,1)S(1)} all-to-all(bf16[8,64,768]{2,1,0:T(8,128)(2,1)} %bitcast.11), channel_id=1, replica_groups=mesh['y'=4,'zhigh'=8,'zlow'=2,'x'=4,'core'=2] {'x','core'}, dimensions={0} | all-to-all | bytes 1572864 | tf_op jit(solution)/shard_map/all_to_all | solution.py:117
  23.5 0.0 copy-start
  23.5 0.0 copy-start.1
  23.5 0.1 convert_reduce_fusion
  23.7 13.6 %all_gather.3.whole = bf16[512,768]{1,0:T(8,128)(2,1)S(1)} all-gather(bf16[64,768]{1,0:T(8,128)(2,1)S(1)} %pad_maximum_fusion), channel_id=1, replica_groups=mesh['y'=4,'zhigh'=8,'zlow'=2,'x'=4,'core'=2] {'x','core'}, dimensions={0}, use_global_device_ids=true | all-gather | bytes 884736 | tf_op jit(solution)/shard_map/all_gather | solution.py:127
  37.3 0.0 copy-done
  37.3 0.0 copy-done.1
  37.3 0.7 back.1
  38.0 21.9 %all_to_all.16 = bf16[8,64,1024]{2,1,0:T(8,128)(2,1)S(1)} all-to-all(bf16[8,64,1024]{2,1,0:T(8,128)(2,1)S(1)} %bitcast.10), channel_id=1, replica_groups=mesh['y'=4,'zhigh'=8,'zlow'=2,'x'=4,'core'=2] {'y','zlow'}, dimensions={0} | all-to-all | bytes 2097152 | tf_op jit(solution)/shard_map/all_to_all | solution.py:117
  60.0 0.0 copy-start.2
  60.0 0.8 reduce_sum.34
  60.8 12.8 %all-to-all-start.2 = ((bf16[8,8,1024]{2,1,0:T(8,128)(2,1)}), bf16[8,8,1024]{2,1,0:T(8,128)(2,1)S(1)}, u32[]{:S(2)}, u32[]{:S(2)}) async-start(bf16[8,8,1024]{2,1,0:T(8,128)(2,1)} %bitcast.2), calls=%async_computation.2 | async-start | bytes 262144 | tf_op jit(solution)/shard_map/all_to_all | solution.py:117
  73.6 0.0 copy-done.2
  73.6 0.5 fusion.4
  74.0 1.0 %copy.11 = bf16[1024,256]{1,0:T(8,128)(2,1)} copy(bf16[1024,256]{0,1:T(8,128)(2,1)S(1)} %fusion.4) | data formatting | bytes 1048576
  75.0 0.0 copy-start.3
  75.0 0.5 fusion.3
  75.5 1.0 %copy.12 = bf16[1024,256]{1,0:T(8,128)(2,1)} copy(bf16[1024,256]{0,1:T(8,128)(2,1)S(1)} %fusion.3) | data formatting | bytes 1048576
  76.5 0.0 copy-done.3
  76.5 1.3 %fusion.2 = bf16[256,1024]{1,0:T(8,128)(2,1)} fusion(bf16[512,1024]{1,0:T(8,128)(2,1)S(1)} %copy-done.3, bf16[512,768]{1,0:T(8,128)(2,1)S(1)} %all_gather.3.whole), kind=kOutput, calls=%fused_computation.6 | convolution fusion | flops 268959744 | bytes 1835008 | tf_op jit(solution)/shard_map/dot_general | solution.py:27
  77.8 11.0 %all-to-all-done.2 = bf16[8,8,1024]{2,1,0:T(8,128)(2,1)S(1)} async-done(((bf16[8,8,1024]{2,1,0:T(8,128)(2,1)}), bf16[8,8,1024]{2,1,0:T(8,128)(2,1)S(1)}, u32[]{:S(2)}, u32[]{:S(2)}) %all-to-all-start.2) | async-done | bytes 131104 | tf_op jit(solution)/shard_map/all_to_all | solution.py:117
  88.7 0.6 reduce_sum.35
  (2 shorter events, 0.1 us)
Async XLA Ops:
  23.5 13.8 %copy-start = (bf16[1024,256]{1,0:T(8,128)(2,1)S(1)}, bf16[1024,256]{1,0:T(8,128)(2,1)}, u32[]{:S(2)}) copy-start(bf16[1024,256]{1,0:T(8,128)(2,1)} %g.1) | copy-start | bytes 1572868
  23.5 13.8 %copy-start.1 = (bf16[1024,256]{1,0:T(8,128)(2,1)S(1)}, bf16[1024,256]{1,0:T(8,128)(2,1)}, u32[]{:S(2)}) copy-start(bf16[1024,256]{1,0:T(8,128)(2,1)} %u.1) | copy-start | bytes 1572868
  60.0 13.6 %copy-start.2 = (bf16[512,1024]{1,0:T(8,128)(2,1)S(1)}, bf16[512,1024]{1,0:T(8,128)(2,1)}, u32[]{:S(2)}) copy-start(bf16[512,1024]{1,0:T(8,128)(2,1)} %x_hbm.1) | copy-start | bytes 3145732
  60.8 28.0 %all-to-all-start.2 = ((bf16[8,8,1024]{2,1,0:T(8,128)(2,1)}), bf16[8,8,1024]{2,1,0:T(8,128)(2,1)S(1)}, u32[]{:S(2)}, u32[]{:S(2)}) async-start(bf16[8,8,1024]{2,1,0:T(8,128)(2,1)} %bitcast.2), calls=%async_computation.2 | async-start | bytes 262144 | tf_op jit(solution)/shard_map/all_to_all | solution.py:117
  75.0 1.5 %copy-start.3 = (bf16[512,1024]{1,0:T(8,128)(2,1)S(1)}, bf16[512,1024]{1,0:T(8,128)(2,1)}, u32[]{:S(2)}) copy-start(bf16[512,1024]{1,0:T(8,128)(2,1)} %o_hbm.1) | copy-start | bytes 3145732

commit v4 on v3

v4 whole, which is shorter than its diff:
```python
import functools
import math

import jax
import jax.numpy as jnp
from jax import lax
from jax.experimental import pallas as pl
from jax.experimental.pallas import tpu as pltpu
from jax.sharding import Mesh, PartitionSpec as P

TOKENS = 512
COL = ("x", "core")
ROW = ("y", "zhigh", "zlow")
NT = (((1,), (1,)), ((), ()))


def swiglu_back(gate, up, act_grad):
    sig = jax.nn.sigmoid(gate)
    hidden = (gate * sig * up).astype(jnp.bfloat16)
    up_grad = (act_grad * gate * sig).astype(jnp.bfloat16)
    gate_grad = (act_grad * up * sig * (1.0 + gate * (1.0 - sig))).astype(jnp.bfloat16)
    return (hidden, gate_grad, up_grad)


def weight_term(left, right, scale):
    return (
        lax.dot_general(left, right, (((0,), (0,)), ((), ())), preferred_element_type=jnp.float32)
        * scale
    ).astype(jnp.bfloat16)


def forward(inputs, out_grad, gate_weight, up_weight, down_weight):
    gate_part = jnp.dot(inputs, gate_weight, preferred_element_type=jnp.float32)
    up_part = jnp.dot(inputs, up_weight, preferred_element_type=jnp.float32)
    act_part = lax.dot_general(out_grad, down_weight, NT, preferred_element_type=jnp.float32)
    return jnp.concatenate([gate_part, up_part, act_part], axis=1).astype(jnp.bfloat16)


def back_kernel(whole, g, u, out):
    units = g.shape[1]
    step = 256
    for j in range(g.shape[0] // step):
        cols = slice(j * step, (j + 1) * step)
        terms = lax.dot_general(
            whole[:, :units], g[cols], NT, preferred_element_type=jnp.float32
        )
        terms += lax.dot_general(
            whole[:, units:], u[cols], NT, preferred_element_type=jnp.float32
        )
        terms = jnp.swapaxes(terms.reshape(4, 8, 2, 8, step), 1, 2)
        out[:, cols] = terms.reshape(-1, step).astype(jnp.bfloat16)


def back(whole, gate_weight, up_weight):
    tokens, width = whole.shape[0], gate_weight.shape[0]
    return pl.pallas_call(
        back_kernel,
        out_shape=jax.ShapeDtypeStruct((tokens, width), jnp.bfloat16),
        in_specs=[pl.BlockSpec(memory_space=pltpu.VMEM)] * 3,
        out_specs=pl.BlockSpec(memory_space=pltpu.VMEM),
        compiler_params=pltpu.CompilerParams(vmem_limit_bytes=24 << 20),
        cost_estimate=pl.CostEstimate(
            flops=4 * tokens * gate_weight.size, bytes_accessed=2500000, transcendentals=0
        ),
        name="back",
    )(whole, gate_weight, up_weight)


def sum_kernel(pieces, out, *, parts):
    terms = pieces[...].astype(jnp.float32)
    out[...] = jnp.sum(terms.reshape((parts, -1) + terms.shape[1:]), axis=0).astype(jnp.bfloat16)


def sum_pieces(pieces):
    parts, rows, width = pieces.shape
    return pl.pallas_call(
        functools.partial(sum_kernel, parts=parts),
        out_shape=jax.ShapeDtypeStruct((rows, width), jnp.bfloat16),
        in_specs=[pl.BlockSpec(memory_space=pltpu.VMEM)],
        out_specs=pl.BlockSpec(memory_space=pltpu.VMEM),
        compiler_params=pltpu.CompilerParams(vmem_limit_bytes=24 << 20),
        name="sum_pieces",
    )(pieces.reshape(parts * rows, width))


def exchange(terms, axis, parts):
    return lax.all_to_all(terms.reshape((parts, -1) + terms.shape[1:]), axis, 0, 0)


def per_device(inputs, out_grad, gate_weight, up_weight, down_weight):
    scale = 1.0 / math.sqrt(TOKENS)
    units = gate_weight.shape[1]
    parts = forward(inputs, out_grad, gate_weight, up_weight, down_weight)
    sums = jnp.sum(exchange(parts, COL, 8).astype(jnp.float32), axis=0)
    own = swiglu_back(sums[:, :units], sums[:, units : 2 * units], sums[:, 2 * units :])
    hidden, gate_grad, up_grad = own
    pair = jnp.concatenate([gate_grad, up_grad], axis=1)
    over_x = lax.all_to_all(jnp.broadcast_to(pair[None], (4,) + pair.shape), "x", 0, 0)
    whole = lax.all_gather(over_x, "core", axis=1).reshape(TOKENS, 2 * units)
    terms = back(whole, gate_weight, up_weight)
    hidden, terms = lax.optimization_barrier((hidden, terms))
    hidden = lax.all_gather(hidden, COL, axis=0, tiled=True)
    near = sum_pieces(exchange(terms, ("y", "zlow"), 8))
    whole, hidden, near = lax.optimization_barrier((whole, hidden, near))
    input_grad = sum_pieces(exchange(near, "zhigh", 8))
    down_wgrad = weight_term(hidden, out_grad, scale)
    gate_wgrad = weight_term(inputs, whole[:, :units], scale)
    up_wgrad = weight_term(inputs, whole[:, units:], scale)
    return (input_grad, gate_wgrad, up_wgrad, down_wgrad)


def solution(mesh):
    grid = Mesh(mesh.devices.reshape(4, 8, 2, 4, 2), ("y", "zhigh", "zlow", "x", "core"))
    return jax.shard_map(
        per_device,
        mesh=grid,
        in_specs=(P(None, COL), P(None, COL), P(COL, ROW), P(COL, ROW), P(ROW, COL)),
        out_specs=(P(ROW, COL), P(COL, ROW), P(COL, ROW), P(ROW, COL)),
        check_vma=False,
    )
```

time: 89.7 us -> 88.3 us (0.984)
  the two profiles are of different devices: /device:TPU:8 before, /device:TPU:2 now
where the time goes in v4:
time: 88.3 us; the launch traced here: 87.8 us
  blocking collectives  43.7 us (49%)
  starting transfers between devices  16.1 us (18%)
  waiting for transfers between devices  14 us (16%)
  matrix products  5.79 us (7%)
  local copies, waits for them, and re-layouts  4.14 us (5%)
  Pallas kernels  3.13 us (4%)
    all_to_all x1, blocking collectives, exchange(): lax.all_to_all(terms.reshape((parts, -1) + terms.shape[1:]), axis, 0, 0)  20.1 us
    all_to_all x2, starting transfers between devices, exchange(): lax.all_to_all(terms.reshape((parts, -1) + terms.shape[1:]), axis, 0, 0)  16.1 us
    all_to_all x2, waiting for transfers between devices, exchange(): lax.all_to_all(terms.reshape((parts, -1) + terms.shape[1:]), axis, 0, 0)  14 us
    all_gather x1, blocking collectives, per_device(): hidden = lax.all_gather(hidden, COL, axis=0, tiled=True)  12.2 us
    all_to_all x1, blocking collectives, per_device(): lax.all_to_all(jnp.broadcast_to(pair[None], (4,) + pair.shape), 'x', 0, 0)  9.19 us
    unnamed x12, local copies, waits for them, and re-layouts  4.12 us
    dot_general x3, matrix products, weight_term(): lax.dot_general(left, right, (((0,), (0,)), ((), ())), preferred_element_...  3.4 us
    all_gather x1, blocking collectives, per_device(): whole = lax.all_gather(over_x, 'core', axis=1).reshape(TOKENS, 2 * units)  2.17 us
  transfers between devices with their start and end apart: 2, of which 2 were waited for; matrix products, arithmetic and copies ran while one was open for 6% of the time, Pallas kernels for 0%

profile of v4, /device:TPU:2, one launch (start us, length us, event | category | flops | bytes accessed | tf_op | source)
XLA Modules:
  0.0 87.8 jit_solution(10335968882412045772)
XLA Ops:
  0.6 0.0 copy-start
  0.6 0.0 copy-start.1
  0.7 1.2 %copy-done = bf16[512,1024]{1,0:T(8,128)(2,1)S(1)} copy-done((bf16[512,1024]{1,0:T(8,128)(2,1)S(1)}, bf16[512,1024]{1,0:T(8,128)(2,1)}, u32[]{:S(2)}) %copy-start) | copy-done | bytes 1048600
  1.9 1.5 %convolution_convert_fusion.2 = bf16[512,256]{1,0:T(8,128)(2,1)S(1)} fusion(bf16[512,1024]{1,0:T(8,128)(2,1)S(1)} %copy-done, bf16[1024,256]{1,0:T(8,128)(2,1)} %g.1), kind=kOutput, calls=%fused_computation.11 | convolution fusion | flops 268566528 | bytes 1835008 | tf_op jit(solution)/shard_map/dot_general | solution.py:33
  3.3 0.0 copy-done.1
  3.4 0.0 copy-start.3
  3.4 0.0 copy-start.4
  3.4 0.4 convolution_convert_fusion.1
  3.8 0.8 copy-done.3
  4.6 0.1 copy-done.4
  4.7 0.5 convolution_convert_fusion
  5.2 0.1 pad_maximum_fusion
  5.3 20.1 %all_to_all.20 = bf16[8,64,768]{2,1,0:T(8,128)(2,1)S(1)} all-to-all(bf16[8,64,768]{2,1,0:T(8,128)(2,1)S(1)} %pad_maximum_fusion), channel_id=1, replica_groups=mesh['y'=4,'zhigh'=8,'zlow'=2,'x'=4,'core'=2] {'x','core'}, dimensions={0} | all-to-all | bytes 1572864 | tf_op jit(solution)/shard_map/all_to_all | solution.py:87
  25.4 0.1 convert_reduce_fusion
  25.5 0.0 copy-start.2
  25.6 9.2 %all_to_all.21 = bf16[4,64,512]{2,1,0:T(8,128)(2,1)S(1)} all-to-all(bf16[4,64,512]{2,1,0:T(8,128)(2,1)S(1)} %broadcast_in_dim.2), channel_id=1, replica_groups=mesh['y'=4,'zhigh'=8,'zlow'=2,'x'=4,'core'=2] {'x'}, dimensions={0} | all-to-all | bytes 524288 | tf_op jit(solution)/shard_map/all_to_all | solution.py:98
  34.8 2.2 %all-gather = bf16[4,128,512]{2,1,0:T(8,128)(2,1)S(1)} all-gather(bf16[4,64,512]{2,1,0:T(8,128)(2,1)S(1)} %all_to_all.21), channel_id=2, replica_groups=mesh['y'=4,'zhigh'=8,'zlow'=2,'x'=4,'core'=2] {'core'}, dimensions={1}, use_global_device_ids=true | all-gather | bytes 786432 | tf_op jit(solution)/shard_map/all_gather | solution.py:99
  36.9 0.0 copy-done.2
  36.9 1.7 %back.1 = bf16[512,1024]{1,0:T(8,128)(2,1)} custom-call(bf16[512,512]{1,0:T(8,128)(2,1)S(1)} %bitcast.23, bf16[1024,256]{1,0:T(8,128)(2,1)S(1)} %copy-done.2, bf16[1024,256]{1,0:T(8,128)(2,1)S(1)} %copy-done.1), custom_call_target="tpu_custom_call" | custom-call | flops 536870912 | bytes 2500000 | tf_op jit(solution)/shard_map/back/pallas_call | solution.py:56
  38.7 3.6 %all-to-all-start.2 = ((bf16[8,64,1024]{2,1,0:T(8,128)(2,1)}), bf16[8,64,1024]{2,1,0:T(8,128)(2,1)S(1)}, u32[]{:S(2)}, u32[]{:S(2)}) async-start(bf16[8,64,1024]{2,1,0:T(8,128)(2,1)} %bitcast.4), calls=%async_computation.2 | async-start | bytes 2097152 | tf_op jit(solution)/shard_map/all_to_all | solution.py:87
  42.2 12.2 %all_gather.11 = bf16[512,256]{1,0:T(8,128)(2,1)S(1)} all-gather(bf16[64,256]{1,0:T(8,128)(2,1)S(1)} %get-tuple-element.9), channel_id=1, replica_groups=mesh['y'=4,'zhigh'=8,'zlow'=2,'x'=4,'core'=2] {'x','core'}, dimensions={0}, use_global_device_ids=true | all-gather | bytes 294912 | tf_op jit(solution)/shard_map/all_gather | solution.py:102
  54.4 4.0 %all-to-all-done.2 = bf16[8,64,1024]{2,1,0:T(8,128)(2,1)S(1)} async-done(((bf16[8,64,1024]{2,1,0:T(8,128)(2,1)}), bf16[8,64,1024]{2,1,0:T(8,128)(2,1)S(1)}, u32[]{:S(2)}, u32[]{:S(2)}) %all-to-all-start.2) | async-done | bytes 1048608 | tf_op jit(solution)/shard_map/all_to_all | solution.py:87
  58.5 0.8 sum_pieces.2
  59.3 12.6 %all-to-all-start.3 = ((bf16[8,8,1024]{2,1,0:T(8,128)(2,1)}), bf16[8,8,1024]{2,1,0:T(8,128)(2,1)S(1)}, u32[]{:S(2)}, u32[]{:S(2)}) async-start(bf16[8,8,1024]{2,1,0:T(8,128)(2,1)} %bitcast.6), calls=%async_computation.3 | async-start | bytes 262144 | tf_op jit(solution)/shard_map/all_to_all | solution.py:87
  71.8 0.5 fusion.4
  72.3 1.0 %copy.9 = bf16[1024,256]{1,0:T(8,128)(2,1)} copy(bf16[1024,256]{0,1:T(8,128)(2,1)S(1)} %fusion.4) | data formatting | bytes 1048576
  73.3 0.5 fusion.3
  73.7 1.0 %copy.10 = bf16[1024,256]{1,0:T(8,128)(2,1)} copy(bf16[1024,256]{0,1:T(8,128)(2,1)S(1)} %fusion.3) | data formatting | bytes 1048576
  74.7 2.5 %fusion.2 = bf16[256,1024]{1,0:T(8,128)(2,1)} fusion(bf16[512,256]{1,0:T(8,128)(2,1)S(1)} %all_gather.11, bf16[512,1024]{1,0:T(8,128)(2,1)} %param.6), kind=kOutput, calls=%fused_computation.6 | convolution fusion | flops 268959744 | bytes 1835008 | tf_op jit(solution)/shard_map/dot_general | solution.py:27
  77.2 10.0 %all-to-all-done.3 = bf16[8,8,1024]{2,1,0:T(8,128)(2,1)S(1)} async-done(((bf16[8,8,1024]{2,1,0:T(8,128)(2,1)}), bf16[8,8,1024]{2,1,0:T(8,128)(2,1)S(1)}, u32[]{:S(2)}, u32[]{:S(2)}) %all-to-all-start.3) | async-done | bytes 131104 | tf_op jit(solution)/shard_map/all_to_all | solution.py:87
  87.2 0.6 sum_pieces.3
  (3 shorter events, 0.1 us)
Async XLA Ops:
  0.6 1.2 %copy-start = (bf16[512,1024]{1,0:T(8,128)(2,1)S(1)}, bf16[512,1024]{1,0:T(8,128)(2,1)}, u32[]{:S(2)}) copy-start(bf16[512,1024]{1,0:T(8,128)(2,1)} %param.5) | copy-start | bytes 3145732
  0.6 2.7 %copy-start.1 = (bf16[1024,256]{1,0:T(8,128)(2,1)S(1)}, bf16[1024,256]{1,0:T(8,128)(2,1)}, u32[]{:S(2)}) copy-start(bf16[1024,256]{1,0:T(8,128)(2,1)} %u.1) | copy-start | bytes 1572868
  3.4 1.2 %copy-start.3 = (bf16[512,1024]{1,0:T(8,128)(2,1)S(1)}, bf16[512,1024]{1,0:T(8,128)(2,1)}, u32[]{:S(2)}) copy-start(bf16[512,1024]{1,0:T(8,128)(2,1)} %param.6) | copy-start | bytes 3145732
  3.4 1.3 %copy-start.4 = (bf16[256,1024]{1,0:T(8,128)(2,1)S(1)}, bf16[256,1024]{1,0:T(8,128)(2,1)}, u32[]{:S(2)}) copy-start(bf16[256,1024]{1,0:T(8,128)(2,1)} %param.9) | copy-start | bytes 1572868
  25.5 11.5 %copy-start.2 = (bf16[1024,256]{1,0:T(8,128)(2,1)S(1)}, bf16[1024,256]{1,0:T(8,128)(2,1)}, u32[]{:S(2)}) copy-start(bf16[1024,256]{1,0:T(8,128)(2,1)} %g.1) | copy-start | bytes 1572868
  38.7 19.8 %all-to-all-start.2 = ((bf16[8,64,1024]{2,1,0:T(8,128)(2,1)}), bf16[8,64,1024]{2,1,0:T(8,128)(2,1)S(1)}, u32[]{:S(2)}, u32[]{:S(2)}) async-start(bf16[8,64,1024]{2,1,0:T(8,128)(2,1)} %bitcast.4), calls=%async_computation.2 | async-start | bytes 2097152 | tf_op jit(solution)/shard_map/all_to_all | solution.py:87
  59.3 27.9 %all-to-all-start.3 = ((bf16[8,8,1024]{2,1,0:T(8,128)(2,1)}), bf16[8,8,1024]{2,1,0:T(8,128)(2,1)S(1)}, u32[]{:S(2)}, u32[]{:S(2)}) async-start(bf16[8,8,1024]{2,1,0:T(8,128)(2,1)} %bitcast.6), calls=%async_computation.3 | async-start | bytes 262144 | tf_op jit(solution)/shard_map/all_to_all | solution.py:87

commit v5 on v4

--- a/solution.py
+++ b/solution.py
@@ -31,24 +31,33 @@
 
 def forward(inputs, out_grad, gate_weight, up_weight, down_weight):
     gate_part = jnp.dot(inputs, gate_weight, preferred_element_type=jnp.float32)
+    out_grad, gate_part = lax.optimization_barrier((out_grad, gate_part))
+    act_part = lax.dot_general(out_grad, down_weight, NT, preferred_element_type=jnp.float32)
+    inputs, act_part = lax.optimization_barrier((inputs, act_part))
     up_part = jnp.dot(inputs, up_weight, preferred_element_type=jnp.float32)
-    act_part = lax.dot_general(out_grad, down_weight, NT, preferred_element_type=jnp.float32)
     return jnp.concatenate([gate_part, up_part, act_part], axis=1).astype(jnp.bfloat16)
 
 
-def back_kernel(whole, g, u, out):
+def back_kernel(whole, g, u, out, terms_vmem, sems):
     units = g.shape[1]
-    step = 256
-    for j in range(g.shape[0] // step):
-        cols = slice(j * step, (j + 1) * step)
-        terms = lax.dot_general(
-            whole[:, :units], g[cols], NT, preferred_element_type=jnp.float32
-        )
-        terms += lax.dot_general(
-            whole[:, units:], u[cols], NT, preferred_element_type=jnp.float32
-        )
-        terms = jnp.swapaxes(terms.reshape(4, 8, 2, 8, step), 1, 2)
-        out[:, cols] = terms.reshape(-1, step).astype(jnp.bfloat16)
+    rows, step = whole.shape[0] // 2, 256
+    copies = []
+    for i in range(2):
+        part = pl.ds(i * rows, rows)
+        for j in range(g.shape[0] // step):
+            cols = pl.ds(j * step, step)
+            terms = lax.dot_general(
+                whole[part, :units], g[cols], NT, preferred_element_type=jnp.float32
+            )
+            terms += lax.dot_general(
+                whole[part, units:], u[cols], NT, preferred_element_type=jnp.float32
+            )
+            terms = jnp.swapaxes(terms.reshape(2, 8, 2, 8, step), 1, 2)
+            terms_vmem[part, cols] = terms.reshape(-1, step).astype(jnp.bfloat16)
+        copies.append(pltpu.make_async_copy(terms_vmem.at[part], out.at[part], sems.at[i]))
+        copies[-1].start()
+    for copy in copies:
+        copy.wait()
 
 
 def back(whole, gate_weight, up_weight):
@@ -57,11 +66,12 @@
         back_kernel,
         out_shape=jax.ShapeDtypeStruct((tokens, width), jnp.bfloat16),
         in_specs=[pl.BlockSpec(memory_space=pltpu.VMEM)] * 3,
-        out_specs=pl.BlockSpec(memory_space=pltpu.VMEM),
+        out_specs=pl.BlockSpec(memory_space=pl.ANY),
+        scratch_shapes=[
+            pltpu.VMEM((tokens, width), jnp.bfloat16),
+            pltpu.SemaphoreType.DMA((width // 256,)),
+        ],
         compiler_params=pltpu.CompilerParams(vmem_limit_bytes=24 << 20),
-        cost_estimate=pl.CostEstimate(
-            flops=4 * tokens * gate_weight.size, bytes_accessed=2500000, transcendentals=0
-        ),
         name="back",
     )(whole, gate_weight, up_weight)
 

time: 88.3 us -> 87.8 us (level)
  no operation moved by 1% of the time
where the time goes in v5:
time: 87.8 us; the launch traced here: 87.4 us
  blocking collectives  43.7 us (50%)
  starting transfers between devices  16.1 us (18%)
  waiting for transfers between devices  14 us (16%)
  matrix products  5.79 us (7%)
  local copies, waits for them, and re-layouts  3.79 us (4%)
  Pallas kernels  2.98 us (3%)
    all_to_all x1, blocking collectives, exchange(): lax.all_to_all(terms.reshape((parts, -1) + terms.shape[1:]), axis, 0, 0)  20.1 us
    all_to_all x2, starting transfers between devices, exchange(): lax.all_to_all(terms.reshape((parts, -1) + terms.shape[1:]), axis, 0, 0)  16.1 us
    all_to_all x2, waiting for transfers between devices, exchange(): lax.all_to_all(terms.reshape((parts, -1) + terms.shape[1:]), axis, 0, 0)  14 us
    all_gather x1, blocking collectives, per_device(): hidden = lax.all_gather(hidden, COL, axis=0, tiled=True)  12.2 us
    all_to_all x1, blocking collectives, per_device(): lax.all_to_all(jnp.broadcast_to(pair[None], (4,) + pair.shape), 'x', 0, 0)  9.19 us
    unnamed x12, local copies, waits for them, and re-layouts  3.77 us
    dot_general x3, matrix products, weight_term(): lax.dot_general(left, right, (((0,), (0,)), ((), ())), preferred_element_...  3.4 us
    all_gather x1, blocking collectives, per_device(): whole = lax.all_gather(over_x, 'core', axis=1).reshape(TOKENS, 2 * units)  2.17 us
  transfers between devices with their start and end apart: 2, of which 2 were waited for; matrix products, arithmetic and copies ran while one was open for 6% of the time, Pallas kernels for 0%

profile of v5, /device:TPU:2, one launch (start us, length us, event | category | flops | bytes accessed | tf_op | source)
XLA Modules:
  0.0 87.4 jit_solution(1735490143004201914)
XLA Ops:
  0.6 0.0 copy-start
  0.6 0.0 copy-start.3
  0.7 0.0 copy-start.4
  0.7 1.2 %copy-done = bf16[512,1024]{1,0:T(8,128)(2,1)S(1)} copy-done((bf16[512,1024]{1,0:T(8,128)(2,1)S(1)}, bf16[512,1024]{1,0:T(8,128)(2,1)}, u32[]{:S(2)}) %copy-start) | copy-done | bytes 1048600
  1.9 1.5 %fusion.7 = bf16[512,256]{1,0:T(8,128)(2,1)S(1)} fusion(bf16[512,1024]{1,0:T(8,128)(2,1)S(1)} %copy-done, bf16[1024,256]{1,0:T(8,128)(2,1)} %g.1), kind=kOutput, calls=%fused_computation.18 | convolution fusion | flops 268435456 | bytes 1835008 | tf_op jit(solution)/shard_map/dot_general | solution.py:33
  3.3 0.0 copy-done.3
  3.4 0.0 copy-done.4
  3.4 0.0 copy-start.1
  3.4 0.5 fusion.8
  3.9 0.6 copy-done.1
  4.4 0.4 convolution_convert_fusion
  4.8 0.1 pad_maximum_fusion
  4.9 20.1 %all_to_all.20 = bf16[8,64,768]{2,1,0:T(8,128)(2,1)S(1)} all-to-all(bf16[8,64,768]{2,1,0:T(8,128)(2,1)S(1)} %pad_maximum_fusion), channel_id=1, replica_groups=mesh['y'=4,'zhigh'=8,'zlow'=2,'x'=4,'core'=2] {'x','core'}, dimensions={0} | all-to-all | bytes 1572864 | tf_op jit(solution)/shard_map/all_to_all | solution.py:97
  25.0 0.1 convert_reduce_fusion
  25.1 0.0 copy-start.2
  25.2 9.2 %all_to_all.21 = bf16[4,64,512]{2,1,0:T(8,128)(2,1)S(1)} all-to-all(bf16[4,64,512]{2,1,0:T(8,128)(2,1)S(1)} %broadcast_in_dim.2), channel_id=1, replica_groups=mesh['y'=4,'zhigh'=8,'zlow'=2,'x'=4,'core'=2] {'x'}, dimensions={0} | all-to-all | bytes 524288 | tf_op jit(solution)/shard_map/all_to_all | solution.py:108
  34.4 2.2 %all-gather = bf16[4,128,512]{2,1,0:T(8,128)(2,1)S(1)} all-gather(bf16[4,64,512]{2,1,0:T(8,128)(2,1)S(1)} %all_to_all.21), channel_id=2, replica_groups=mesh['y'=4,'zhigh'=8,'zlow'=2,'x'=4,'core'=2] {'core'}, dimensions={1}, use_global_device_ids=true | all-gather | bytes 786432 | tf_op jit(solution)/shard_map/all_gather | solution.py:109
  36.6 0.0 copy-done.2
  36.6 1.6 %back.1 = bf16[512,1024]{1,0:T(8,128)(2,1)} custom-call(bf16[512,512]{1,0:T(8,128)(2,1)S(1)} %bitcast.23, bf16[1024,256]{1,0:T(8,128)(2,1)S(1)} %copy-done.2, bf16[1024,256]{1,0:T(8,128)(2,1)S(1)} %copy-done.1), custom_call_target="tpu_custom_call" | custom-call | tf_op jit(solution)/shard_map/back/pallas_call | solution.py:65
  38.2 3.6 %all-to-all-start.2 = ((bf16[8,64,1024]{2,1,0:T(8,128)(2,1)}), bf16[8,64,1024]{2,1,0:T(8,128)(2,1)S(1)}, u32[]{:S(2)}, u32[]{:S(2)}) async-start(bf16[8,64,1024]{2,1,0:T(8,128)(2,1)} %bitcast.4), calls=%async_computation.2 | async-start | bytes 2097152 | tf_op jit(solution)/shard_map/all_to_all | solution.py:97
  41.8 12.2 %all_gather.11 = bf16[512,256]{1,0:T(8,128)(2,1)S(1)} all-gather(bf16[64,256]{1,0:T(8,128)(2,1)S(1)} %get-tuple-element.17), channel_id=1, replica_groups=mesh['y'=4,'zhigh'=8,'zlow'=2,'x'=4,'core'=2] {'x','core'}, dimensions={0}, use_global_device_ids=true | all-gather | bytes 294912 | tf_op jit(solution)/shard_map/all_gather | solution.py:112
  54.0 4.0 %all-to-all-done.2 = bf16[8,64,1024]{2,1,0:T(8,128)(2,1)S(1)} async-done(((bf16[8,64,1024]{2,1,0:T(8,128)(2,1)}), bf16[8,64,1024]{2,1,0:T(8,128)(2,1)S(1)}, u32[]{:S(2)}, u32[]{:S(2)}) %all-to-all-start.2) | async-done | bytes 1048608 | tf_op jit(solution)/shard_map/all_to_all | solution.py:97
  58.0 0.8 sum_pieces.2
  58.8 12.5 %all-to-all-start.3 = ((bf16[8,8,1024]{2,1,0:T(8,128)(2,1)}), bf16[8,8,1024]{2,1,0:T(8,128)(2,1)S(1)}, u32[]{:S(2)}, u32[]{:S(2)}) async-start(bf16[8,8,1024]{2,1,0:T(8,128)(2,1)} %bitcast.6), calls=%async_computation.3 | async-start | bytes 262144 | tf_op jit(solution)/shard_map/all_to_all | solution.py:97
  71.4 0.5 fusion.4
  71.8 1.0 %copy.9 = bf16[1024,256]{1,0:T(8,128)(2,1)} copy(bf16[1024,256]{0,1:T(8,128)(2,1)S(1)} %fusion.4) | data formatting | bytes 1048576
  72.8 0.5 fusion.3
  73.3 1.0 %copy.10 = bf16[1024,256]{1,0:T(8,128)(2,1)} copy(bf16[1024,256]{0,1:T(8,128)(2,1)S(1)} %fusion.3) | data formatting | bytes 1048576
  74.3 2.5 %fusion.2 = bf16[256,1024]{1,0:T(8,128)(2,1)} fusion(bf16[512,256]{1,0:T(8,128)(2,1)S(1)} %all_gather.11, bf16[512,1024]{1,0:T(8,128)(2,1)} %param.6), kind=kOutput, calls=%fused_computation.6 | convolution fusion | flops 268959744 | bytes 1835008 | tf_op jit(solution)/shard_map/dot_general | solution.py:27
  76.8 10.0 %all-to-all-done.3 = bf16[8,8,1024]{2,1,0:T(8,128)(2,1)S(1)} async-done(((bf16[8,8,1024]{2,1,0:T(8,128)(2,1)}), bf16[8,8,1024]{2,1,0:T(8,128)(2,1)S(1)}, u32[]{:S(2)}, u32[]{:S(2)}) %all-to-all-start.3) | async-done | bytes 131104 | tf_op jit(solution)/shard_map/all_to_all | solution.py:97
  86.7 0.6 sum_pieces.3
  (3 shorter events, 0.1 us)
Async XLA Ops:
  0.6 1.2 %copy-start = (bf16[512,1024]{1,0:T(8,128)(2,1)S(1)}, bf16[512,1024]{1,0:T(8,128)(2,1)}, u32[]{:S(2)}) copy-start(bf16[512,1024]{1,0:T(8,128)(2,1)} %param.5) | copy-start | bytes 3145732
  0.6 2.7 %copy-start.3 = (bf16[512,1024]{1,0:T(8,128)(2,1)S(1)}, bf16[512,1024]{1,0:T(8,128)(2,1)}, u32[]{:S(2)}) copy-start(bf16[512,1024]{1,0:T(8,128)(2,1)} %param.6) | copy-start | bytes 3145732
  0.7 2.7 %copy-start.4 = (bf16[256,1024]{1,0:T(8,128)(2,1)S(1)}, bf16[256,1024]{1,0:T(8,128)(2,1)}, u32[]{:S(2)}) copy-start(bf16[256,1024]{1,0:T(8,128)(2,1)} %param.9) | copy-start | bytes 1572868
  3.4 1.0 %copy-start.1 = (bf16[1024,256]{1,0:T(8,128)(2,1)S(1)}, bf16[1024,256]{1,0:T(8,128)(2,1)}, u32[]{:S(2)}) copy-start(bf16[1024,256]{1,0:T(8,128)(2,1)} %u.1) | copy-start | bytes 1572868
  25.1 11.5 %copy-start.2 = (bf16[1024,256]{1,0:T(8,128)(2,1)S(1)}, bf16[1024,256]{1,0:T(8,128)(2,1)}, u32[]{:S(2)}) copy-start(bf16[1024,256]{1,0:T(8,128)(2,1)} %g.1) | copy-start | bytes 1572868
  38.2 19.8 %all-to-all-start.2 = ((bf16[8,64,1024]{2,1,0:T(8,128)(2,1)}), bf16[8,64,1024]{2,1,0:T(8,128)(2,1)S(1)}, u32[]{:S(2)}, u32[]{:S(2)}) async-start(bf16[8,64,1024]{2,1,0:T(8,128)(2,1)} %bitcast.4), calls=%async_computation.2 | async-start | bytes 2097152 | tf_op jit(solution)/shard_map/all_to_all | solution.py:97
  58.8 27.9 %all-to-all-start.3 = ((bf16[8,8,1024]{2,1,0:T(8,128)(2,1)}), bf16[8,8,1024]{2,1,0:T(8,128)(2,1)S(1)}, u32[]{:S(2)}, u32[]{:S(2)}) async-start(bf16[8,8,1024]{2,1,0:T(8,128)(2,1)} %bitcast.6), calls=%async_computation.3 | async-start | bytes 262144 | tf_op jit(solution)/shard_map/all_to_all | solution.py:97

commit v6 on v4

--- a/solution.py
+++ b/solution.py
@@ -31,8 +31,10 @@
 
 def forward(inputs, out_grad, gate_weight, up_weight, down_weight):
     gate_part = jnp.dot(inputs, gate_weight, preferred_element_type=jnp.float32)
+    out_grad, gate_part = lax.optimization_barrier((out_grad, gate_part))
+    act_part = lax.dot_general(out_grad, down_weight, NT, preferred_element_type=jnp.float32)
+    inputs, act_part = lax.optimization_barrier((inputs, act_part))
     up_part = jnp.dot(inputs, up_weight, preferred_element_type=jnp.float32)
-    act_part = lax.dot_general(out_grad, down_weight, NT, preferred_element_type=jnp.float32)
     return jnp.concatenate([gate_part, up_part, act_part], axis=1).astype(jnp.bfloat16)
 
 
@@ -42,10 +44,10 @@
     for j in range(g.shape[0] // step):
         cols = slice(j * step, (j + 1) * step)
         terms = lax.dot_general(
-            whole[:, :units], g[cols], NT, preferred_element_type=jnp.float32
+            whole[:, units : 2 * units], g[cols], NT, preferred_element_type=jnp.float32
         )
         terms += lax.dot_general(
-            whole[:, units:], u[cols], NT, preferred_element_type=jnp.float32
+            whole[:, 2 * units :], u[cols], NT, preferred_element_type=jnp.float32
         )
         terms = jnp.swapaxes(terms.reshape(4, 8, 2, 8, step), 1, 2)
         out[:, cols] = terms.reshape(-1, step).astype(jnp.bfloat16)
@@ -93,19 +95,16 @@
     parts = forward(inputs, out_grad, gate_weight, up_weight, down_weight)
     sums = jnp.sum(exchange(parts, COL, 8).astype(jnp.float32), axis=0)
     own = swiglu_back(sums[:, :units], sums[:, units : 2 * units], sums[:, 2 * units :])
-    hidden, gate_grad, up_grad = own
-    pair = jnp.concatenate([gate_grad, up_grad], axis=1)
-    over_x = lax.all_to_all(jnp.broadcast_to(pair[None], (4,) + pair.shape), "x", 0, 0)
-    whole = lax.all_gather(over_x, "core", axis=1).reshape(TOKENS, 2 * units)
+    own = jnp.concatenate(own, axis=1)
+    over_x = lax.all_to_all(jnp.broadcast_to(own[None], (4,) + own.shape), "x", 0, 0)
+    whole = lax.all_gather(over_x, "core", axis=1).reshape(TOKENS, 3 * units)
     terms = back(whole, gate_weight, up_weight)
-    hidden, terms = lax.optimization_barrier((hidden, terms))
-    hidden = lax.all_gather(hidden, COL, axis=0, tiled=True)
     near = sum_pieces(exchange(terms, ("y", "zlow"), 8))
-    whole, hidden, near = lax.optimization_barrier((whole, hidden, near))
+    whole, near = lax.optimization_barrier((whole, near))
     input_grad = sum_pieces(exchange(near, "zhigh", 8))
-    down_wgrad = weight_term(hidden, out_grad, scale)
-    gate_wgrad = weight_term(inputs, whole[:, :units], scale)
-    up_wgrad = weight_term(inputs, whole[:, units:], scale)
+    down_wgrad = weight_term(whole[:, :units], out_grad, scale)
+    gate_wgrad = weight_term(inputs, whole[:, units : 2 * units], scale)
+    up_wgrad = weight_term(inputs, whole[:, 2 * units :], scale)
     return (input_grad, gate_wgrad, up_wgrad, down_wgrad)
 
 

time: 88.3 us -> 88 us (level)
  blocking collectives: 43.7 us -> 51.7 us
  waiting for transfers between devices: 14 us -> 11.1 us
  starting transfers between devices: 16.1 us -> 13.4 us
  matrix products: 5.79 us -> 4.56 us
  Pallas kernels: 3.13 us -> 2.15 us
    all_to_all x1 -> x2, blocking collectives: 20.1 us -> 38.8 us  [exchange(): lax.all_to_all(terms.reshape((parts, -1) + terms.shape[1:]), axis, 0, 0)]
    all_gather x2 -> x1, blocking collectives: 14.4 us -> 2.36 us  [per_device(): whole = lax.all_gather(over_x, 'core', axis=1).reshape(TOKENS, 3 * units)]
    all_to_all x2 -> x1, waiting for transfers between devices: 14 us -> 11.1 us  [exchange(): lax.all_to_all(terms.reshape((parts, -1) + terms.shape[1:]), axis, 0, 0)]
    all_to_all x2 -> x1, starting transfers between devices: 16.1 us -> 13.4 us  [exchange(): lax.all_to_all(terms.reshape((parts, -1) + terms.shape[1:]), axis, 0, 0)]
    all_to_all x1, blocking collectives: 9.19 us -> 10.5 us  [per_device(): lax.all_to_all(jnp.broadcast_to(own[None], (4,) + own.shape), 'x', 0, 0)]
    dot_general x3, matrix products: 3.4 us -> 2.18 us  [weight_term(): lax.dot_general(left, right, (((0,), (0,)), ((), ())), preferred_element_...]
    pallas_call x1, Pallas kernels: 1.71 us -> 0.74 us  [back(): pl.pallas_call(back_kernel, out_shape=jax.ShapeDtypeStruct((tokens, width...]
  transfers between devices with their start and end apart: 2 -> 1, of which waited for: 2 -> 1; matrix products, arithmetic and copies ran while one was open for 6% -> 5% of each run, Pallas kernels for 0% -> 0%
where the time goes in v6:
time: 88 us; the launch traced here: 87.6 us
  blocking collectives  51.7 us (59%)
  starting transfers between devices  13.4 us (15%)
  waiting for transfers between devices  11.1 us (13%)
  matrix products  4.56 us (5%)
  local copies, waits for them, and re-layouts  3.8 us (4%)
  Pallas kernels  2.15 us (2%)
    all_to_all x2, blocking collectives, exchange(): lax.all_to_all(terms.reshape((parts, -1) + terms.shape[1:]), axis, 0, 0)  38.8 us
    all_to_all x1, starting transfers between devices, exchange(): lax.all_to_all(terms.reshape((parts, -1) + terms.shape[1:]), axis, 0, 0)  13.4 us
    all_to_all x1, waiting for transfers between devices, exchange(): lax.all_to_all(terms.reshape((parts, -1) + terms.shape[1:]), axis, 0, 0)  11.1 us
    all_to_all x1, blocking collectives, per_device(): lax.all_to_all(jnp.broadcast_to(own[None], (4,) + own.shape), 'x', 0, 0)  10.5 us
    unnamed x12, local copies, waits for them, and re-layouts  3.77 us
    all_gather x1, blocking collectives, per_device(): whole = lax.all_gather(over_x, 'core', axis=1).reshape(TOKENS, 3 * units)  2.36 us
    dot_general x3, matrix products, weight_term(): lax.dot_general(left, right, (((0,), (0,)), ((), ())), preferred_element_...  2.18 us
  transfers between devices with their start and end apart: 1, of which 1 were waited for; matrix products, arithmetic and copies ran while one was open for 5% of the time, Pallas kernels for 0%

profile of v6, /device:TPU:2, one launch (start us, length us, event | category | flops | bytes accessed | tf_op | source)
XLA Modules:
  0.0 87.6 jit_solution(11145953878516435211)
XLA Ops:
  0.6 0.0 copy-start
  0.6 0.0 copy-start.3
  0.7 0.0 copy-start.4
  0.7 1.2 %copy-done = bf16[512,1024]{1,0:T(8,128)(2,1)S(1)} copy-done((bf16[512,1024]{1,0:T(8,128)(2,1)S(1)}, bf16[512,1024]{1,0:T(8,128)(2,1)}, u32[]{:S(2)}) %copy-start) | copy-done | bytes 1048600
  1.9 1.5 %fusion.8 = bf16[512,256]{1,0:T(8,128)(2,1)S(1)} fusion(bf16[512,1024]{1,0:T(8,128)(2,1)S(1)} %copy-done, bf16[1024,256]{1,0:T(8,128)(2,1)} %g.1), kind=kOutput, calls=%fused_computation.19 | convolution fusion | flops 268435456 | bytes 1835008 | tf_op jit(solution)/shard_map/dot_general | solution.py:33
  3.3 0.0 copy-done.3
  3.4 0.0 copy-done.4
  3.4 0.0 copy-start.1
  3.4 0.5 fusion.9
  3.9 0.6 copy-done.1
  4.4 0.4 convolution_convert_fusion
  4.8 0.1 pad_maximum_fusion
  4.9 20.1 %all_to_all.20 = bf16[8,64,768]{2,1,0:T(8,128)(2,1)S(1)} all-to-all(bf16[8,64,768]{2,1,0:T(8,128)(2,1)S(1)} %pad_maximum_fusion), channel_id=1, replica_groups=mesh['y'=4,'zhigh'=8,'zlow'=2,'x'=4,'core'=2] {'x','core'}, dimensions={0} | all-to-all | bytes 1572864 | tf_op jit(solution)/shard_map/all_to_all | solution.py:89
  25.0 0.1 convert_reduce_fusion
  25.2 0.0 copy-start.2
  25.2 10.5 %all_to_all.21 = bf16[4,64,768]{2,1,0:T(8,128)(2,1)S(1)} all-to-all(bf16[4,64,768]{2,1,0:T(8,128)(2,1)S(1)} %broadcast_in_dim.2), channel_id=1, replica_groups=mesh['y'=4,'zhigh'=8,'zlow'=2,'x'=4,'core'=2] {'x'}, dimensions={0} | all-to-all | bytes 786432 | tf_op jit(solution)/shard_map/all_to_all | solution.py:99
  35.8 2.4 %all-gather = bf16[4,128,768]{2,1,0:T(8,128)(2,1)S(1)} all-gather(bf16[4,64,768]{2,1,0:T(8,128)(2,1)S(1)} %all_to_all.21), channel_id=2, replica_groups=mesh['y'=4,'zhigh'=8,'zlow'=2,'x'=4,'core'=2] {'core'}, dimensions={1}, use_global_device_ids=true | all-gather | bytes 1179648 | tf_op jit(solution)/shard_map/all_gather | solution.py:100
  38.1 0.0 copy-done.2
  38.1 0.7 back.1
  38.9 18.7 %all_to_all.22 = bf16[8,64,1024]{2,1,0:T(8,128)(2,1)S(1)} all-to-all(bf16[8,64,1024]{2,1,0:T(8,128)(2,1)S(1)} %bitcast.22), channel_id=1, replica_groups=mesh['y'=4,'zhigh'=8,'zlow'=2,'x'=4,'core'=2] {'y','zlow'}, dimensions={0} | all-to-all | bytes 2097152 | tf_op jit(solution)/shard_map/all_to_all | solution.py:89
  57.6 0.8 sum_pieces.2
  58.3 13.4 %all-to-all-start.3 = ((bf16[8,8,1024]{2,1,0:T(8,128)(2,1)}), bf16[8,8,1024]{2,1,0:T(8,128)(2,1)S(1)}, u32[]{:S(2)}, u32[]{:S(2)}) async-start(bf16[8,8,1024]{2,1,0:T(8,128)(2,1)} %bitcast.6), calls=%async_computation.3 | async-start | bytes 262144 | tf_op jit(solution)/shard_map/all_to_all | solution.py:89
  71.8 0.5 fusion.4
  72.2 1.0 %copy.9 = bf16[1024,256]{1,0:T(8,128)(2,1)} copy(bf16[1024,256]{0,1:T(8,128)(2,1)S(1)} %fusion.4) | data formatting | bytes 1048576
  73.2 0.5 fusion.3
  73.7 1.0 %copy.10 = bf16[1024,256]{1,0:T(8,128)(2,1)} copy(bf16[1024,256]{0,1:T(8,128)(2,1)S(1)} %fusion.3) | data formatting | bytes 1048576
  74.7 1.3 %fusion.2 = bf16[256,1024]{1,0:T(8,128)(2,1)} fusion(bf16[512,1024]{1,0:T(8,128)(2,1)S(1)} %copy-done.3, bf16[512,768]{1,0:T(8,128)(2,1)S(1)} %bitcast.26), kind=kOutput, calls=%fused_computation.6 | convolution fusion | flops 268959744 | bytes 1835008 | tf_op jit(solution)/shard_map/dot_general | solution.py:27
  76.0 11.1 %all-to-all-done.3 = bf16[8,8,1024]{2,1,0:T(8,128)(2,1)S(1)} async-done(((bf16[8,8,1024]{2,1,0:T(8,128)(2,1)}), bf16[8,8,1024]{2,1,0:T(8,128)(2,1)S(1)}, u32[]{:S(2)}, u32[]{:S(2)}) %all-to-all-start.3) | async-done | bytes 131104 | tf_op jit(solution)/shard_map/all_to_all | solution.py:89
  87.0 0.6 sum_pieces.3
  (3 shorter events, 0.1 us)
Async XLA Ops:
  0.6 1.2 %copy-start = (bf16[512,1024]{1,0:T(8,128)(2,1)S(1)}, bf16[512,1024]{1,0:T(8,128)(2,1)}, u32[]{:S(2)}) copy-start(bf16[512,1024]{1,0:T(8,128)(2,1)} %param.5) | copy-start | bytes 3145732
  0.6 2.7 %copy-start.3 = (bf16[512,1024]{1,0:T(8,128)(2,1)S(1)}, bf16[512,1024]{1,0:T(8,128)(2,1)}, u32[]{:S(2)}) copy-start(bf16[512,1024]{1,0:T(8,128)(2,1)} %param.6) | copy-start | bytes 3145732
  0.7 2.7 %copy-start.4 = (bf16[256,1024]{1,0:T(8,128)(2,1)S(1)}, bf16[256,1024]{1,0:T(8,128)(2,1)}, u32[]{:S(2)}) copy-start(bf16[256,1024]{1,0:T(8,128)(2,1)} %param.9) | copy-start | bytes 1572868
  3.4 1.0 %copy-start.1 = (bf16[1024,256]{1,0:T(8,128)(2,1)S(1)}, bf16[1024,256]{1,0:T(8,128)(2,1)}, u32[]{:S(2)}) copy-start(bf16[1024,256]{1,0:T(8,128)(2,1)} %u.1) | copy-start | bytes 1572868
  25.2 12.9 %copy-start.2 = (bf16[1024,256]{1,0:T(8,128)(2,1)S(1)}, bf16[1024,256]{1,0:T(8,128)(2,1)}, u32[]{:S(2)}) copy-start(bf16[1024,256]{1,0:T(8,128)(2,1)} %g.1) | copy-start | bytes 1572868
  58.3 28.7 %all-to-all-start.3 = ((bf16[8,8,1024]{2,1,0:T(8,128)(2,1)}), bf16[8,8,1024]{2,1,0:T(8,128)(2,1)S(1)}, u32[]{:S(2)}, u32[]{:S(2)}) async-start(bf16[8,8,1024]{2,1,0:T(8,128)(2,1)} %bitcast.6), calls=%async_computation.3 | async-start | bytes 262144 | tf_op jit(solution)/shard_map/all_to_all | solution.py:89

commit v7 on v5

--- a/solution.py
+++ b/solution.py
@@ -77,8 +77,20 @@
 
 
 def sum_kernel(pieces, out, *, parts):
-    terms = pieces[...].astype(jnp.float32)
-    out[...] = jnp.sum(terms.reshape((parts, -1) + terms.shape[1:]), axis=0).astype(jnp.bfloat16)
+    rows = pieces.shape[0] // parts
+    step = 16
+    if rows % step == 0:
+        for r in range(0, rows, step):
+            total = pieces[r : r + step].astype(jnp.float32)
+            for p in range(1, parts):
+                total += pieces[p * rows + r : p * rows + r + step].astype(jnp.float32)
+            out[r : r + step] = total.astype(jnp.bfloat16)
+    else:
+        total = pieces[:step].astype(jnp.float32)
+        for r in range(step, pieces.shape[0], step):
+            total += pieces[r : r + step].astype(jnp.float32)
+        total = jnp.sum(total.reshape((step // rows, rows) + total.shape[1:]), axis=0)
+        out[...] = total.astype(jnp.bfloat16)
 
 
 def sum_pieces(pieces):

time: 87.8 us -> 87.8 us (level)
  no operation moved by 1% of the time
where the time goes in v7:
time: 87.8 us; the launch traced here: 87.4 us
  blocking collectives  43.7 us (50%)
  starting transfers between devices  16.1 us (18%)
  waiting for transfers between devices  14 us (16%)
  matrix products  5.79 us (7%)
  local copies, waits for them, and re-layouts  3.79 us (4%)
  Pallas kernels  2.98 us (3%)
    all_to_all x1, blocking collectives, exchange(): lax.all_to_all(terms.reshape((parts, -1) + terms.shape[1:]), axis, 0, 0)  20.1 us
    all_to_all x2, starting transfers between devices, exchange(): lax.all_to_all(terms.reshape((parts, -1) + terms.shape[1:]), axis, 0, 0)  16.1 us
    all_to_all x2, waiting for transfers between devices, exchange(): lax.all_to_all(terms.reshape((parts, -1) + terms.shape[1:]), axis, 0, 0)  14 us
    all_gather x1, blocking collectives, per_device(): hidden = lax.all_gather(hidden, COL, axis=0, tiled=True)  12.2 us
    all_to_all x1, blocking collectives, per_device(): lax.all_to_all(jnp.broadcast_to(pair[None], (4,) + pair.shape), 'x', 0, 0)  9.19 us
    unnamed x12, local copies, waits for them, and re-layouts  3.77 us
    dot_general x3, matrix products, weight_term(): lax.dot_general(left, right, (((0,), (0,)), ((), ())), preferred_element_...  3.4 us
    all_gather x1, blocking collectives, per_device(): whole = lax.all_gather(over_x, 'core', axis=1).reshape(TOKENS, 2 * units)  2.17 us
  transfers between devices with their start and end apart: 2, of which 2 were waited for; matrix products, arithmetic and copies ran while one was open for 6% of the time, Pallas kernels for 0%

profile of v7, /device:TPU:2, one launch (start us, length us, event | category | flops | bytes accessed | tf_op | source)
XLA Modules:
  0.0 87.4 jit_solution(739263553443744136)
XLA Ops:
  0.6 0.0 copy-start
  0.6 0.0 copy-start.3
  0.7 0.0 copy-start.4
  0.7 1.2 %copy-done = bf16[512,1024]{1,0:T(8,128)(2,1)S(1)} copy-done((bf16[512,1024]{1,0:T(8,128)(2,1)S(1)}, bf16[512,1024]{1,0:T(8,128)(2,1)}, u32[]{:S(2)}) %copy-start) | copy-done | bytes 1048600
  1.9 1.5 %fusion.7 = bf16[512,256]{1,0:T(8,128)(2,1)S(1)} fusion(bf16[512,1024]{1,0:T(8,128)(2,1)S(1)} %copy-done, bf16[1024,256]{1,0:T(8,128)(2,1)} %g.1), kind=kOutput, calls=%fused_computation.18 | convolution fusion | flops 268435456 | bytes 1835008 | tf_op jit(solution)/shard_map/dot_general | solution.py:33
  3.3 0.0 copy-done.3
  3.4 0.0 copy-done.4
  3.4 0.0 copy-start.1
  3.4 0.5 fusion.8
  3.9 0.6 copy-done.1
  4.4 0.4 convolution_convert_fusion
  4.8 0.1 pad_maximum_fusion
  4.9 20.1 %all_to_all.20 = bf16[8,64,768]{2,1,0:T(8,128)(2,1)S(1)} all-to-all(bf16[8,64,768]{2,1,0:T(8,128)(2,1)S(1)} %pad_maximum_fusion), channel_id=1, replica_groups=mesh['y'=4,'zhigh'=8,'zlow'=2,'x'=4,'core'=2] {'x','core'}, dimensions={0} | all-to-all | bytes 1572864 | tf_op jit(solution)/shard_map/all_to_all | solution.py:109
  25.0 0.1 convert_reduce_fusion
  25.1 0.0 copy-start.2
  25.2 9.2 %all_to_all.21 = bf16[4,64,512]{2,1,0:T(8,128)(2,1)S(1)} all-to-all(bf16[4,64,512]{2,1,0:T(8,128)(2,1)S(1)} %broadcast_in_dim.2), channel_id=1, replica_groups=mesh['y'=4,'zhigh'=8,'zlow'=2,'x'=4,'core'=2] {'x'}, dimensions={0} | all-to-all | bytes 524288 | tf_op jit(solution)/shard_map/all_to_all | solution.py:120
  34.4 2.2 %all-gather = bf16[4,128,512]{2,1,0:T(8,128)(2,1)S(1)} all-gather(bf16[4,64,512]{2,1,0:T(8,128)(2,1)S(1)} %all_to_all.21), channel_id=2, replica_groups=mesh['y'=4,'zhigh'=8,'zlow'=2,'x'=4,'core'=2] {'core'}, dimensions={1}, use_global_device_ids=true | all-gather | bytes 786432 | tf_op jit(solution)/shard_map/all_gather | solution.py:121
  36.6 0.0 copy-done.2
  36.6 1.6 %back.1 = bf16[512,1024]{1,0:T(8,128)(2,1)} custom-call(bf16[512,512]{1,0:T(8,128)(2,1)S(1)} %bitcast.23, bf16[1024,256]{1,0:T(8,128)(2,1)S(1)} %copy-done.2, bf16[1024,256]{1,0:T(8,128)(2,1)S(1)} %copy-done.1), custom_call_target="tpu_custom_call" | custom-call | tf_op jit(solution)/shard_map/back/pallas_call | solution.py:65
  38.2 3.6 %all-to-all-start.2 = ((bf16[8,64,1024]{2,1,0:T(8,128)(2,1)}), bf16[8,64,1024]{2,1,0:T(8,128)(2,1)S(1)}, u32[]{:S(2)}, u32[]{:S(2)}) async-start(bf16[8,64,1024]{2,1,0:T(8,128)(2,1)} %bitcast.4), calls=%async_computation.2 | async-start | bytes 2097152 | tf_op jit(solution)/shard_map/all_to_all | solution.py:109
  41.8 12.2 %all_gather.11 = bf16[512,256]{1,0:T(8,128)(2,1)S(1)} all-gather(bf16[64,256]{1,0:T(8,128)(2,1)S(1)} %get-tuple-element.17), channel_id=1, replica_groups=mesh['y'=4,'zhigh'=8,'zlow'=2,'x'=4,'core'=2] {'x','core'}, dimensions={0}, use_global_device_ids=true | all-gather | bytes 294912 | tf_op jit(solution)/shard_map/all_gather | solution.py:124
  54.0 4.0 %all-to-all-done.2 = bf16[8,64,1024]{2,1,0:T(8,128)(2,1)S(1)} async-done(((bf16[8,64,1024]{2,1,0:T(8,128)(2,1)}), bf16[8,64,1024]{2,1,0:T(8,128)(2,1)S(1)}, u32[]{:S(2)}, u32[]{:S(2)}) %all-to-all-start.2) | async-done | bytes 1048608 | tf_op jit(solution)/shard_map/all_to_all | solution.py:109
  58.0 0.8 sum_pieces.2
  58.8 12.5 %all-to-all-start.3 = ((bf16[8,8,1024]{2,1,0:T(8,128)(2,1)}), bf16[8,8,1024]{2,1,0:T(8,128)(2,1)S(1)}, u32[]{:S(2)}, u32[]{:S(2)}) async-start(bf16[8,8,1024]{2,1,0:T(8,128)(2,1)} %bitcast.6), calls=%async_computation.3 | async-start | bytes 262144 | tf_op jit(solution)/shard_map/all_to_all | solution.py:109
  71.4 0.5 fusion.4
  71.8 1.0 %copy.9 = bf16[1024,256]{1,0:T(8,128)(2,1)} copy(bf16[1024,256]{0,1:T(8,128)(2,1)S(1)} %fusion.4) | data formatting | bytes 1048576
  72.8 0.5 fusion.3
  73.3 1.0 %copy.10 = bf16[1024,256]{1,0:T(8,128)(2,1)} copy(bf16[1024,256]{0,1:T(8,128)(2,1)S(1)} %fusion.3) | data formatting | bytes 1048576
  74.3 2.5 %fusion.2 = bf16[256,1024]{1,0:T(8,128)(2,1)} fusion(bf16[512,256]{1,0:T(8,128)(2,1)S(1)} %all_gather.11, bf16[512,1024]{1,0:T(8,128)(2,1)} %param.6), kind=kOutput, calls=%fused_computation.6 | convolution fusion | flops 268959744 | bytes 1835008 | tf_op jit(solution)/shard_map/dot_general | solution.py:27
  76.8 10.0 %all-to-all-done.3 = bf16[8,8,1024]{2,1,0:T(8,128)(2,1)S(1)} async-done(((bf16[8,8,1024]{2,1,0:T(8,128)(2,1)}), bf16[8,8,1024]{2,1,0:T(8,128)(2,1)S(1)}, u32[]{:S(2)}, u32[]{:S(2)}) %all-to-all-start.3) | async-done | bytes 131104 | tf_op jit(solution)/shard_map/all_to_all | solution.py:109
  86.7 0.6 sum_pieces.3
  (3 shorter events, 0.1 us)
Async XLA Ops:
  0.6 1.2 %copy-start = (bf16[512,1024]{1,0:T(8,128)(2,1)S(1)}, bf16[512,1024]{1,0:T(8,128)(2,1)}, u32[]{:S(2)}) copy-start(bf16[512,1024]{1,0:T(8,128)(2,1)} %param.5) | copy-start | bytes 3145732
  0.6 2.7 %copy-start.3 = (bf16[512,1024]{1,0:T(8,128)(2,1)S(1)}, bf16[512,1024]{1,0:T(8,128)(2,1)}, u32[]{:S(2)}) copy-start(bf16[512,1024]{1,0:T(8,128)(2,1)} %param.6) | copy-start | bytes 3145732
  0.7 2.7 %copy-start.4 = (bf16[256,1024]{1,0:T(8,128)(2,1)S(1)}, bf16[256,1024]{1,0:T(8,128)(2,1)}, u32[]{:S(2)}) copy-start(bf16[256,1024]{1,0:T(8,128)(2,1)} %param.9) | copy-start | bytes 1572868
  3.4 1.0 %copy-start.1 = (bf16[1024,256]{1,0:T(8,128)(2,1)S(1)}, bf16[1024,256]{1,0:T(8,128)(2,1)}, u32[]{:S(2)}) copy-start(bf16[1024,256]{1,0:T(8,128)(2,1)} %u.1) | copy-start | bytes 1572868
  25.1 11.5 %copy-start.2 = (bf16[1024,256]{1,0:T(8,128)(2,1)S(1)}, bf16[1024,256]{1,0:T(8,128)(2,1)}, u32[]{:S(2)}) copy-start(bf16[1024,256]{1,0:T(8,128)(2,1)} %g.1) | copy-start | bytes 1572868
  38.2 19.8 %all-to-all-start.2 = ((bf16[8,64,1024]{2,1,0:T(8,128)(2,1)}), bf16[8,64,1024]{2,1,0:T(8,128)(2,1)S(1)}, u32[]{:S(2)}, u32[]{:S(2)}) async-start(bf16[8,64,1024]{2,1,0:T(8,128)(2,1)} %bitcast.4), calls=%async_computation.2 | async-start | bytes 2097152 | tf_op jit(solution)/shard_map/all_to_all | solution.py:109
  58.8 27.9 %all-to-all-start.3 = ((bf16[8,8,1024]{2,1,0:T(8,128)(2,1)}), bf16[8,8,1024]{2,1,0:T(8,128)(2,1)S(1)}, u32[]{:S(2)}, u32[]{:S(2)}) async-start(bf16[8,8,1024]{2,1,0:T(8,128)(2,1)} %bitcast.6), calls=%async_computation.3 | async-start | bytes 262144 | tf_op jit(solution)/shard_map/all_to_all | solution.py:109
